TPU v7x, 128 devices: a whole 4x4x4 slice. The times are simulated.
128 devices in a mesh: segment: 8 (over x_lo, z), dp: 16 (over x_hi, y, core).
Axes of the slice: x: 4 (x_hi: 2, x_lo: 2; x = x_hi * 2 + x_lo), y: 4, z: 4, core: 2. Of those that a mesh axis runs over, the one named last changes fastest.
Arguments:
- control_in: bfloat16 [4096, 1536], P('dp'), may hold values from -10 to 10
- base_in: bfloat16 [4096, 2560], P('dp'), may hold values from -6 to 6
- base_update: bfloat16 [8, 4096, 2560], P('segment', 'dp'), may hold values from -4 to 4
- out_gain: float32 [2560], replicated, may hold values from 0.25 to 1.75
- cotangent: bfloat16 [4096, 2560], P('dp'), may hold values from -6 to 6
- w_qkv: bfloat16 [8, 1536, 2304], P('segment', 'dp'), may hold values from -1 to 1
- w_out: bfloat16 [8, 768, 1536], P('segment', 'dp'), may hold values from -0.21875 to 0.21875
- w_hint: bfloat16 [8, 1536, 2560], P('segment', 'dp'), may hold values from -0.15625 to 0.15625
- window_offset: int32 [8, 4], P('segment'), may hold values from -1 to 1
- tile_mask: int32 [8, 4, 4], P('segment'), may hold values 0 or 1
- token_layout: int32 [16, 256], P('dp'), may hold values from 0 to 255, each once within a row
Outputs:
- features: float32 [4096, 2560], P('dp')
- grad_qkv: float32 [8, 1536, 2304], P('segment', 'dp')
- grad_out: float32 [8, 768, 1536], P('segment', 'dp')
- grad_hint: float32 [8, 1536, 2560], P('segment', 'dp')
All inputs are finite; a program needn't handle non-finite values. No bound on the sum of `tile_mask` on one device may be relied on, other than what follows from the above.
Results may differ from a plain program's by a relative error of at most 0.03.
Values may be sent and summed in bfloat16 or wider, within the bound.
A program may use at most 192 MiB of HBM per device.

v0:
```python
import jax
import jax.numpy as jnp
from jax import lax
from jax.sharding import PartitionSpec as P

HEADS = 6
HEAD = 128
TILE = 64


def passed_along(value, axis, by):
    size = lax.axis_size(axis)
    pairs = [(i, i + by) for i in range(size) if 0 <= i + by < size]
    return lax.ppermute(value, axis, pairs)


def token_mask(offset, mask):
    count = mask.shape[0]
    row_tile = jnp.arange(count)[:, None]
    col_tile = jnp.arange(count)[None, :]
    near_window = jnp.abs(col_tile - row_tile - offset[:, None]) <= 1
    permitted = (row_tile == col_tile) | near_window & (mask == 1)
    return jnp.repeat(jnp.repeat(permitted, TILE, 0), TILE, 1)


def flat_positions(layout):
    count, length = layout.shape
    return (layout + (jnp.arange(count) * length)[:, None]).reshape(-1)


def forward_block(control, positions, permitted, weight_qkv, weight_out, weight_hint):
    total_rows = control.shape[0]
    length = permitted.shape[0]
    count = total_rows // length
    widened = control.astype(jnp.float32)
    inverse = lax.rsqrt(jnp.mean(widened * widened, -1, keepdims=True) + 1e-06)
    normed = (widened * inverse).astype(jnp.bfloat16)
    projected = jnp.dot(normed, weight_qkv, preferred_element_type=jnp.float32).astype(jnp.bfloat16)
    tiled_proj = projected[positions].reshape(count, length, 3, HEADS, HEAD)
    query_rows = tiled_proj[:, :, 0]
    key_rows = tiled_proj[:, :, 1]
    value_rows = tiled_proj[:, :, 2]
    scores = jnp.einsum(
        "cqhe,ckhe->chqk", query_rows, key_rows, preferred_element_type=jnp.float32
    ) * HEAD ** (-0.5)
    scores = jnp.where(permitted, scores, -1e30)
    row_max = jnp.max(scores, -1, keepdims=True)
    shifted = jnp.exp(scores - row_max)
    softmax_out = shifted / jnp.sum(shifted, -1, keepdims=True)
    soft_half = softmax_out.astype(jnp.bfloat16)
    attended = jnp.einsum(
        "chqk,ckhe->cqhe", soft_half, value_rows, preferred_element_type=jnp.float32
    ).astype(jnp.bfloat16)
    attended = attended.reshape(total_rows, HEADS * HEAD)
    merged = jnp.zeros_like(attended).at[positions].set(attended)
    control_out = (
        widened + jnp.dot(merged, weight_out, preferred_element_type=jnp.float32)
    ).astype(jnp.bfloat16)
    hint_term = jnp.dot(control_out, weight_hint, preferred_element_type=jnp.float32)
    return (control_out, hint_term, (control, normed, tiled_proj, softmax_out, merged))


def backward_block(
    saved, control_out, grad_next, grad_summed, positions, weight_qkv, weight_out, weight_hint
):
    control, normed, tiled_proj, softmax_out, merged = saved
    total_rows = control.shape[0]
    count, length = (tiled_proj.shape[0], tiled_proj.shape[1])
    grad_after = (
        grad_next.astype(jnp.float32)
        + jnp.dot(grad_summed, weight_hint.T, preferred_element_type=jnp.float32)
    ).astype(jnp.bfloat16)
    grad_hint = jnp.dot(control_out.T, grad_summed, preferred_element_type=jnp.float32)
    grad_out = jnp.dot(merged.T, grad_after, preferred_element_type=jnp.float32)
    grad_merged = jnp.dot(grad_after, weight_out.T, preferred_element_type=jnp.float32).astype(
        jnp.bfloat16
    )
    grad_tiled = grad_merged[positions].reshape(count, length, HEADS, HEAD)
    query_rows = tiled_proj[:, :, 0]
    key_rows = tiled_proj[:, :, 1]
    value_rows = tiled_proj[:, :, 2]
    soft_half = softmax_out.astype(jnp.bfloat16)
    grad_values = jnp.einsum(
        "chqk,cqhe->ckhe", soft_half, grad_tiled, preferred_element_type=jnp.float32
    ).astype(jnp.bfloat16)
    grad_probs = jnp.einsum(
        "cqhe,ckhe->chqk", grad_tiled, value_rows, preferred_element_type=jnp.float32
    )
    grad_scores = (
        softmax_out
        * (grad_probs - jnp.sum(grad_probs * softmax_out, -1, keepdims=True))
        * HEAD ** (-0.5)
    )
    grad_scores = grad_scores.astype(jnp.bfloat16)
    grad_queries = jnp.einsum(
        "chqk,ckhe->cqhe", grad_scores, key_rows, preferred_element_type=jnp.float32
    ).astype(jnp.bfloat16)
    grad_keys = jnp.einsum(
        "chqk,cqhe->ckhe", grad_scores, query_rows, preferred_element_type=jnp.float32
    ).astype(jnp.bfloat16)
    grad_stack = jnp.stack((grad_queries, grad_keys, grad_values), 2).reshape(
        total_rows, 3 * HEADS * HEAD
    )
    grad_proj = jnp.zeros_like(grad_stack).at[positions].set(grad_stack)
    grad_qkv = jnp.dot(normed.T, grad_proj, preferred_element_type=jnp.float32)
    grad_normed = jnp.dot(grad_proj, weight_qkv.T, preferred_element_type=jnp.float32)
    widened = control.astype(jnp.float32)
    inverse = lax.rsqrt(jnp.mean(widened * widened, -1, keepdims=True) + 1e-06)
    through = inverse * grad_normed - widened * inverse**3 * jnp.mean(
        grad_normed * widened, -1, keepdims=True
    )
    grad_control = (grad_after.astype(jnp.float32) + through).astype(jnp.bfloat16)
    return (grad_control, (grad_qkv, grad_out, grad_hint))


def norm_grad(summed, gain, cotangent):
    inverse = lax.rsqrt(jnp.mean(summed * summed, -1, keepdims=True) + 1e-06)
    features = summed * inverse * gain
    grad_normed = cotangent.astype(jnp.float32) * gain
    grad_summed = inverse * grad_normed - summed * inverse**3 * jnp.mean(
        grad_normed * summed, -1, keepdims=True
    )
    return (features, grad_summed.astype(jnp.bfloat16))


def shards(
    control_in,
    base_in,
    base_update,
    out_gain,
    cotangent,
    w_qkv,
    w_out,
    w_hint,
    window_offset,
    tile_mask,
    token_layout,
):
    segments = lax.axis_size("segment")
    mine = lax.axis_index("segment")
    weight_qkv, weight_out, weight_hint = (
        lax.all_gather(w_qkv[0], "dp", axis=0, tiled=True),
        lax.all_gather(w_out[0], "dp", axis=0, tiled=True),
        lax.all_gather(w_hint[0], "dp", axis=0, tiled=True),
    )
    permitted = token_mask(window_offset[0], tile_mask[0])
    total_rows, width = control_in.shape
    count, length = token_layout.shape
    feat_width = base_in.shape[1]
    factor = float(total_rows * lax.axis_size("dp")) ** (-0.5)
    positions = flat_positions(token_layout)
    empty_state = (
        jnp.zeros((total_rows, width), jnp.bfloat16),
        jnp.zeros((total_rows, width), jnp.bfloat16),
        jnp.zeros((count, length, 3, HEADS, HEAD), jnp.bfloat16),
        jnp.zeros((count, HEADS, length, length), jnp.float32),
        jnp.zeros((total_rows, HEADS * HEAD), jnp.bfloat16),
    )
    empty_out = jnp.zeros((total_rows, width), jnp.bfloat16)
    empty_hint = jnp.zeros((total_rows, feat_width), jnp.float32)

    def run_forward(carry):
        control_out, hint_term, saved = forward_block(
            carry[0], positions, permitted, weight_qkv, weight_out, weight_hint
        )
        return (control_out, saved, control_out, hint_term)

    def keep_forward(carry):
        return carry

    def forward_turn(tick, carry):
        result = lax.cond(mine == tick, run_forward, keep_forward, carry)
        passed = passed_along(result[0], "segment", 1)
        return (passed,) + result[1:]

    carry = lax.fori_loop(
        0, segments, forward_turn, (control_in, empty_state, empty_out, empty_hint)
    )
    saved, control_out, hint_term = (carry[1], carry[2], carry[3])
    term = base_update[0].astype(jnp.float32) + hint_term
    summed = base_in.astype(jnp.float32) + lax.psum(term.astype(jnp.bfloat16), "segment").astype(
        jnp.float32
    )
    features, grad_summed = norm_grad(summed, out_gain, cotangent)
    empty_grads = (
        jnp.zeros(weight_qkv.shape, jnp.float32),
        jnp.zeros(weight_out.shape, jnp.float32),
        jnp.zeros(weight_hint.shape, jnp.float32),
    )

    def run_backward(carry_back):
        return backward_block(
            saved,
            control_out,
            carry_back[0],
            grad_summed,
            positions,
            weight_qkv,
            weight_out,
            weight_hint,
        )

    def keep_backward(carry_back):
        return carry_back

    def backward_turn(tick, carry_back):
        result = lax.cond(mine == segments - 1 - tick, run_backward, keep_backward, carry_back)
        passed = passed_along(result[0], "segment", -1)
        return (passed, result[1])

    start_back = (jnp.zeros((total_rows, width), jnp.bfloat16), empty_grads)
    local_grads = lax.fori_loop(0, segments, backward_turn, start_back)[1]
    summed_grads = (
        lax.psum_scatter(
            local_grads[0].astype(jnp.bfloat16), "dp", scatter_dimension=0, tiled=True
        ).astype(jnp.float32),
        lax.psum_scatter(
            local_grads[1].astype(jnp.bfloat16), "dp", scatter_dimension=0, tiled=True
        ).astype(jnp.float32),
        lax.psum_scatter(
            local_grads[2].astype(jnp.bfloat16), "dp", scatter_dimension=0, tiled=True
        ).astype(jnp.float32),
    )
    return (
        features,
        (summed_grads[0] * factor)[None],
        (summed_grads[1] * factor)[None],
        (summed_grads[2] * factor)[None],
    )


def solution(mesh):
    placed = (
        P("dp", None),
        P("dp", None),
        P("segment", "dp", None),
        P(),
        P("dp", None),
        P("segment", "dp", None),
        P("segment", "dp", None),
        P("segment", "dp", None),
        P("segment", None),
        P("segment", None, None),
        P("dp", None),
    )
    return jax.shard_map(
        shards,
        mesh=mesh,
        in_specs=placed,
        out_specs=(
            P("dp", None),
            P("segment", "dp", None),
            P("segment", "dp", None),
            P("segment", "dp", None),
        ),
        check_vma=False,
    )
```

profile of v0, /device:TPU:1, one launch (start us, length us, event | category | flops | bytes accessed | tf_op | source)
XLA Modules:
  0.0 1467.5 jit_solution(2682473131936568013)
XLA Ops:
  10.3 52.1 %all-gather.9.cloned.1.call-done = bf16[1,768,1536]{2,1,0:T(8,128)(2,1)} async-done(((bf16[1,48,1536]{2,1,0:T(8,128)(2,1)}), bf16[1,768,1536]{2,1,0:T(8,128)(2,1)}) %all-gather.9.cloned.1.call-update) | async-done | bytes 2359312 | tf_op jit(solution)/shard_map/all_gather | solution.py:143
  62.4 68.6 %all-gather.7.cloned.1.call-done = bf16[1,1536,2304]{2,1,0:T(8,128)(2,1)} async-done(((bf16[1,96,2304]{2,1,0:T(8,128)(2,1)}), bf16[1,1536,2304]{2,1,0:T(8,128)(2,1)}) %all-gather.7.cloned.1.call-update) | async-done | bytes 7077904 | tf_op jit(solution)/shard_map/all_gather | solution.py:142
  131.1 71.0 %all-gather.11.cloned.1.call-done = bf16[1,1536,2560]{2,1,0:T(8,128)(2,1)} async-done(((bf16[1,96,2560]{2,1,0:T(8,128)(2,1)}), bf16[1,1536,2560]{2,1,0:T(8,128)(2,1)}) %all-gather.11.cloned.1.call-update) | async-done | bytes 7864336 | tf_op jit(solution)/shard_map/all_gather | solution.py:144
  207.7 309.2 %while.48 = (s32[]{:T(128)}, bf16[256,1536]{1,0:T(8,128)(2,1)S(1)}, bf16[256,1536]{1,0:T(8,128)(2,1)}, bf16[256,1536]{1,0:T(8,128)(2,1)}, bf16[1,256,3,6,128]{1,...) while((s32[]{:T(128)}, bf16[256,1536]{1,0:T(8,128)(2,1)S(1)}, ...), condition=%wide.region_7.8_spmd.clone, body=%wide.region_0.7_spmd.clone.sunk | while | flops 4739436544 | bytes 56196560 | solution.py:176
  209.0 30.6 %conditional.6 = (bf16[256,1536]{1,0:T(8,128)(2,1)}, bf16[256,1536]{1,0:T(8,128)(2,1)}, bf16[256,1536]{1,0:T(8,128)(2,1)}, bf16[1,256,3,6,128]{1,4,3,2,0:T(8,128...) conditional(s32[]{:T(128)} %convert_element_type.230, ...), branch_computations={%region_1.0_spmd, %region_2.6_spmd} | conditional | flops 4739436544 | bytes 52983960 | solution.py:172
  241.0 17.3 %collective-permute-done.1 = bf16[256,1536]{1,0:T(8,128)(2,1)S(1)} collective-permute-done((bf16[256,1536]{1,0:T(8,128)(2,1)}, bf16[256,1536]{1,0:T(8,128)(2,1)S(1)}, u32[]{:S(2)}, u32[]{:S(2)}) %collective-permute-start.1) | collective-permute-done | bytes 786464 | tf_op jit(solution)/shard_map/while/body/eval_jaxpr/ppermute | solution.py:14
  260.4 33.8 %collective-permute-start.1 = (bf16[256,1536]{1,0:T(8,128)(2,1)}, bf16[256,1536]{1,0:T(8,128)(2,1)S(1)}, u32[]{:S(2)}, u32[]{:S(2)}) collective-permute-start(bf16[256,1536]{1,0:T(8,128)(2,1)} %get-tuple-element.999), channel_id=1, source_target_pairs={{0,16},{16,32},{32,48},{48,64},{64,80},{80,96},{96,112},{1,17},{17... | collective-permute-start | bytes 2359304 | tf_op jit(solution)/shard_map/while/body/eval_jaxpr/ppermute | solution.py:14
  294.2 16.4 %collective-permute-done.1 = bf16[256,1536]{1,0:T(8,128)(2,1)S(1)} collective-permute-done((bf16[256,1536]{1,0:T(8,128)(2,1)}, bf16[256,1536]{1,0:T(8,128)(2,1)S(1)}, u32[]{:S(2)}, u32[]{:S(2)}) %collective-permute-start.1) | collective-permute-done | bytes 786464 | tf_op jit(solution)/shard_map/while/body/eval_jaxpr/ppermute | solution.py:14
  316.8 15.5 %collective-permute-done.1 = bf16[256,1536]{1,0:T(8,128)(2,1)S(1)} collective-permute-done((bf16[256,1536]{1,0:T(8,128)(2,1)}, bf16[256,1536]{1,0:T(8,128)(2,1)S(1)}, u32[]{:S(2)}, u32[]{:S(2)}) %collective-permute-start.1) | collective-permute-done | bytes 786464 | tf_op jit(solution)/shard_map/while/body/eval_jaxpr/ppermute | solution.py:14
  334.4 32.3 %collective-permute-start.1 = (bf16[256,1536]{1,0:T(8,128)(2,1)}, bf16[256,1536]{1,0:T(8,128)(2,1)S(1)}, u32[]{:S(2)}, u32[]{:S(2)}) collective-permute-start(bf16[256,1536]{1,0:T(8,128)(2,1)} %get-tuple-element.999), channel_id=1, source_target_pairs={{0,16},{16,32},{32,48},{48,64},{64,80},{80,96},{96,112},{1,17},{17... | collective-permute-start | bytes 2359304 | tf_op jit(solution)/shard_map/while/body/eval_jaxpr/ppermute | solution.py:14
  366.7 14.8 %collective-permute-done.1 = bf16[256,1536]{1,0:T(8,128)(2,1)S(1)} collective-permute-done((bf16[256,1536]{1,0:T(8,128)(2,1)}, bf16[256,1536]{1,0:T(8,128)(2,1)S(1)}, u32[]{:S(2)}, u32[]{:S(2)}) %collective-permute-start.1) | collective-permute-done | bytes 786464 | tf_op jit(solution)/shard_map/while/body/eval_jaxpr/ppermute | solution.py:14
  387.7 13.9 collective-permute-done.1
  403.8 32.5 %collective-permute-start.1 = (bf16[256,1536]{1,0:T(8,128)(2,1)}, bf16[256,1536]{1,0:T(8,128)(2,1)S(1)}, u32[]{:S(2)}, u32[]{:S(2)}) collective-permute-start(bf16[256,1536]{1,0:T(8,128)(2,1)} %get-tuple-element.999), channel_id=1, source_target_pairs={{0,16},{16,32},{32,48},{48,64},{64,80},{80,96},{96,112},{1,17},{17... | collective-permute-start | bytes 2359304 | tf_op jit(solution)/shard_map/while/body/eval_jaxpr/ppermute | solution.py:14
  436.4 13.3 collective-permute-done.1
  455.9 12.4 collective-permute-done.1
  470.4 34.9 %collective-permute-start.1 = (bf16[256,1536]{1,0:T(8,128)(2,1)}, bf16[256,1536]{1,0:T(8,128)(2,1)S(1)}, u32[]{:S(2)}, u32[]{:S(2)}) collective-permute-start(bf16[256,1536]{1,0:T(8,128)(2,1)} %get-tuple-element.999), channel_id=1, source_target_pairs={{0,16},{16,32},{32,48},{48,64},{64,80},{80,96},{96,112},{1,17},{17... | collective-permute-start | bytes 2359304 | tf_op jit(solution)/shard_map/while/body/eval_jaxpr/ppermute | solution.py:14
  505.2 11.7 collective-permute-done.1
  522.2 166.9 %all-reduce.2.cloned.1.call-done = bf16[256,2560]{1,0:T(8,128)(2,1)} async-done(((bf16[256,2560]{1,0:T(8,128)(2,1)}), bf16[256,2560]{1,0:T(8,128)(2,1)}) %all-reduce.2.cloned.1.call-update) | async-done | bytes 1310736 | tf_op jit(solution)/shard_map/psum | solution.py:181
  705.1 472.9 %while.47 = (s32[]{:T(128)}, bf16[256,1536]{1,0:T(8,128)(2,1)}, bf16[1536,2304]{0,1:T(8,128)(2,1)}, bf16[768,1536]{0,1:T(8,128)(2,1)}, bf16[1536,2560]{1,0:T(8,1...) while((s32[]{:T(128)}, bf16[256,1536]{1,0:T(8,128)(2,1)}, ...), condition=%wide.region_18.19_spmd, body=%wide.region_11.18_spmd.sunk | while | flops 9272034304 | bytes 100301824 | solution.py:212
  706.4 14.1 collective-permute-done
  722.8 13.8 collective-permute-done
  738.8 14.0 collective-permute-done
  755.0 14.7 collective-permute-done
  771.8 14.3 collective-permute-done
  788.3 14.0 collective-permute-done
  804.5 314.4 %collective-permute-done = bf16[256,1536]{1,0:T(8,128)(2,1)S(1)} collective-permute-done((bf16[256,1536]{1,0:T(8,128)(2,1)}, bf16[256,1536]{1,0:T(8,128)(2,1)S(1)}, u32[]{:S(2)}, u32[]{:S(2)}) %collective-permute-start) | collective-permute-done | bytes 786464 | tf_op jit(solution)/shard_map/while/body/eval_jaxpr/ppermute | solution.py:14
  1119.9 44.3 %conditional.5 = ((bf16[256,1536]{1,0:T(8,128)(2,1)}, bf16[1536,2304]{0,1:T(8,128)(2,1)}, bf16[768,1536]{0,1:T(8,128)(2,1)}, bf16[1536,2560]{1,0:T(8,128)(2,1)})) conditional(s32[]{:T(128)} %convert_element_type.229, (bf16[256,1536]{1,0:T(8,128)(2,1)}, bf16[1536,2304]{0,1:T(8,128)(2,1)}, bf16[768,1536]{0,1:T(8,128)(2,1)}, ...), branch_computations={%region_12.12_spmd, %region_13.17_spmd} | conditional | flops 9272034304 | bytes 95582864 | solution.py:207
  1165.5 11.6 collective-permute-done
  1182.4 10.1 copy.43
  1193.2 68.0 %reduce-scatter.6.cloned.1.call-done = bf16[48,1536]{1,0:T(8,128)(2,1)} async-done(((bf16[768,1536]{1,0:T(8,128)(2,1)}), bf16[48,1536]{1,0:T(8,128)(2,1)}) %reduce-scatter.6.cloned.1.call-update) | async-done | bytes 147472 | tf_op jit(solution)/shard_map/reduce_scatter | solution.py:217
  1262.9 95.6 %reduce-scatter.4.cloned.1.call-done = bf16[96,2304]{1,0:T(8,128)(2,1)} async-done(((bf16[1536,2304]{1,0:T(8,128)(2,1)}), bf16[96,2304]{1,0:T(8,128)(2,1)}) %reduce-scatter.4.cloned.1.call-update) | async-done | bytes 442384 | tf_op jit(solution)/shard_map/reduce_scatter | solution.py:214
  1360.5 98.1 %reduce-scatter.8.cloned.1.call-done = bf16[96,2560]{1,0:T(8,128)(2,1)} async-done(((bf16[1536,2560]{1,0:T(8,128)(2,1)}), bf16[96,2560]{1,0:T(8,128)(2,1)}) %reduce-scatter.8.cloned.1.call-update) | async-done | bytes 491536 | tf_op jit(solution)/shard_map/reduce_scatter | solution.py:220
  (155 shorter events, 169.2 us)
Async XLA Ops:
  7.2 2.3 copy-start.13
  7.2 2.3 copy-start.12
  7.2 55.2 %all-gather.9.cloned.1.call-start = ((), (), s32[]{:S(2)}) async-start(), calls=%async_computation.8 | async-start | bytes 2506752 | tf_op jit(solution)/shard_map/all_gather | solution.py:143
  7.9 123.1 %all-gather.7.cloned.1.call-start = ((), (), s32[]{:S(2)}) async-start(), calls=%async_computation.7 | async-start | bytes 7520256 | tf_op jit(solution)/shard_map/all_gather | solution.py:142
  8.7 193.4 %all-gather.11.cloned.1.call-start = ((), (), s32[]{:S(2)}) async-start(), calls=%async_computation.9 | async-start | bytes 8355840 | tf_op jit(solution)/shard_map/all_gather | solution.py:144
  9.4 679.7 %all-reduce.2.cloned.1.call-start = ((), (), s32[]{:S(2)}) async-start(), calls=%async_computation.3 | async-start | bytes 2621440 | tf_op jit(solution)/shard_map/psum | solution.py:181
  217.7 2.8 copy-start.7
  239.6 18.6 %collective-permute-start.1 = (bf16[256,1536]{1,0:T(8,128)(2,1)}, bf16[256,1536]{1,0:T(8,128)(2,1)S(1)}, u32[]{:S(2)}, u32[]{:S(2)}) collective-permute-start(bf16[256,1536]{1,0:T(8,128)(2,1)} %get-tuple-element.999), channel_id=1, source_target_pairs={{0,16},{16,32},{32,48},{48,64},{64,80},{80,96},{96,112},{1,17},{17... | collective-permute-start | bytes 2359304 | tf_op jit(solution)/shard_map/while/body/eval_jaxpr/ppermute | solution.py:14
  260.4 50.2 %collective-permute-start.1 = (bf16[256,1536]{1,0:T(8,128)(2,1)}, bf16[256,1536]{1,0:T(8,128)(2,1)S(1)}, u32[]{:S(2)}, u32[]{:S(2)}) collective-permute-start(bf16[256,1536]{1,0:T(8,128)(2,1)} %get-tuple-element.999), channel_id=1, source_target_pairs={{0,16},{16,32},{32,48},{48,64},{64,80},{80,96},{96,112},{1,17},{17... | collective-permute-start | bytes 2359304 | tf_op jit(solution)/shard_map/while/body/eval_jaxpr/ppermute | solution.py:14
  312.7 19.5 %collective-permute-start.1 = (bf16[256,1536]{1,0:T(8,128)(2,1)}, bf16[256,1536]{1,0:T(8,128)(2,1)S(1)}, u32[]{:S(2)}, u32[]{:S(2)}) collective-permute-start(bf16[256,1536]{1,0:T(8,128)(2,1)} %get-tuple-element.999), channel_id=1, source_target_pairs={{0,16},{16,32},{32,48},{48,64},{64,80},{80,96},{96,112},{1,17},{17... | collective-permute-start | bytes 2359304 | tf_op jit(solution)/shard_map/while/body/eval_jaxpr/ppermute | solution.py:14
  334.4 47.2 %collective-permute-start.1 = (bf16[256,1536]{1,0:T(8,128)(2,1)}, bf16[256,1536]{1,0:T(8,128)(2,1)S(1)}, u32[]{:S(2)}, u32[]{:S(2)}) collective-permute-start(bf16[256,1536]{1,0:T(8,128)(2,1)} %get-tuple-element.999), channel_id=1, source_target_pairs={{0,16},{16,32},{32,48},{48,64},{64,80},{80,96},{96,112},{1,17},{17... | collective-permute-start | bytes 2359304 | tf_op jit(solution)/shard_map/while/body/eval_jaxpr/ppermute | solution.py:14
  383.7 18.0 %collective-permute-start.1 = (bf16[256,1536]{1,0:T(8,128)(2,1)}, bf16[256,1536]{1,0:T(8,128)(2,1)S(1)}, u32[]{:S(2)}, u32[]{:S(2)}) collective-permute-start(bf16[256,1536]{1,0:T(8,128)(2,1)} %get-tuple-element.999), channel_id=1, source_target_pairs={{0,16},{16,32},{32,48},{48,64},{64,80},{80,96},{96,112},{1,17},{17... | collective-permute-start | bytes 2359304 | tf_op jit(solution)/shard_map/while/body/eval_jaxpr/ppermute | solution.py:14
  403.8 45.8 %collective-permute-start.1 = (bf16[256,1536]{1,0:T(8,128)(2,1)}, bf16[256,1536]{1,0:T(8,128)(2,1)S(1)}, u32[]{:S(2)}, u32[]{:S(2)}) collective-permute-start(bf16[256,1536]{1,0:T(8,128)(2,1)} %get-tuple-element.999), channel_id=1, source_target_pairs={{0,16},{16,32},{32,48},{48,64},{64,80},{80,96},{96,112},{1,17},{17... | collective-permute-start | bytes 2359304 | tf_op jit(solution)/shard_map/while/body/eval_jaxpr/ppermute | solution.py:14
  451.8 16.4 %collective-permute-start.1 = (bf16[256,1536]{1,0:T(8,128)(2,1)}, bf16[256,1536]{1,0:T(8,128)(2,1)S(1)}, u32[]{:S(2)}, u32[]{:S(2)}) collective-permute-start(bf16[256,1536]{1,0:T(8,128)(2,1)} %get-tuple-element.999), channel_id=1, source_target_pairs={{0,16},{16,32},{32,48},{48,64},{64,80},{80,96},{96,112},{1,17},{17... | collective-permute-start | bytes 2359304 | tf_op jit(solution)/shard_map/while/body/eval_jaxpr/ppermute | solution.py:14
  470.4 46.6 %collective-permute-start.1 = (bf16[256,1536]{1,0:T(8,128)(2,1)}, bf16[256,1536]{1,0:T(8,128)(2,1)S(1)}, u32[]{:S(2)}, u32[]{:S(2)}) collective-permute-start(bf16[256,1536]{1,0:T(8,128)(2,1)} %get-tuple-element.999), channel_id=1, source_target_pairs={{0,16},{16,32},{32,48},{48,64},{64,80},{80,96},{96,112},{1,17},{17... | collective-permute-start | bytes 2359304 | tf_op jit(solution)/shard_map/while/body/eval_jaxpr/ppermute | solution.py:14
  520.5 168.6 %copy-start.11 = (f32[2560]{0:T(1024)S(1)}, f32[2560]{0:T(1024)}, u32[]{:S(2)}) copy-start(f32[2560]{0:T(1024)} %param.22) | copy-start | bytes 30724
  520.5 740.7 %reduce-scatter.6.cloned.1.call-start = ((), (), s32[]{:S(2)}) async-start(), calls=%async_computation.5 | async-start | bytes 2506752 | tf_op jit(solution)/shard_map/reduce_scatter | solution.py:217
  689.1 3.1 copy-start.4
  689.1 3.1 copy-start.5
  689.1 3.3 copy-start.6
  705.1 15.4 %collective-permute-start = (bf16[256,1536]{1,0:T(8,128)(2,1)}, bf16[256,1536]{1,0:T(8,128)(2,1)S(1)}, u32[]{:S(2)}, u32[]{:S(2)}) collective-permute-start(bf16[256,1536]{1,0:T(8,128)(2,1)} %get-tuple-element.980), channel_id=1, source_target_pairs={{16,0},{32,16},{48,32},{64,48},{80,64},{96,80},{112,96},{17,1},{33... | collective-permute-start | bytes 2359304 | tf_op jit(solution)/shard_map/while/body/eval_jaxpr/ppermute | solution.py:14
  721.5 15.1 %collective-permute-start = (bf16[256,1536]{1,0:T(8,128)(2,1)}, bf16[256,1536]{1,0:T(8,128)(2,1)S(1)}, u32[]{:S(2)}, u32[]{:S(2)}) collective-permute-start(bf16[256,1536]{1,0:T(8,128)(2,1)} %get-tuple-element.980), channel_id=1, source_target_pairs={{16,0},{32,16},{48,32},{64,48},{80,64},{96,80},{112,96},{17,1},{33... | collective-permute-start | bytes 2359304 | tf_op jit(solution)/shard_map/while/body/eval_jaxpr/ppermute | solution.py:14
  737.5 15.3 %collective-permute-start = (bf16[256,1536]{1,0:T(8,128)(2,1)}, bf16[256,1536]{1,0:T(8,128)(2,1)S(1)}, u32[]{:S(2)}, u32[]{:S(2)}) collective-permute-start(bf16[256,1536]{1,0:T(8,128)(2,1)} %get-tuple-element.980), channel_id=1, source_target_pairs={{16,0},{32,16},{48,32},{64,48},{80,64},{96,80},{112,96},{17,1},{33... | collective-permute-start | bytes 2359304 | tf_op jit(solution)/shard_map/while/body/eval_jaxpr/ppermute | solution.py:14
  753.7 15.9 %collective-permute-start = (bf16[256,1536]{1,0:T(8,128)(2,1)}, bf16[256,1536]{1,0:T(8,128)(2,1)S(1)}, u32[]{:S(2)}, u32[]{:S(2)}) collective-permute-start(bf16[256,1536]{1,0:T(8,128)(2,1)} %get-tuple-element.980), channel_id=1, source_target_pairs={{16,0},{32,16},{48,32},{64,48},{80,64},{96,80},{112,96},{17,1},{33... | collective-permute-start | bytes 2359304 | tf_op jit(solution)/shard_map/while/body/eval_jaxpr/ppermute | solution.py:14
  770.6 15.6 %collective-permute-start = (bf16[256,1536]{1,0:T(8,128)(2,1)}, bf16[256,1536]{1,0:T(8,128)(2,1)S(1)}, u32[]{:S(2)}, u32[]{:S(2)}) collective-permute-start(bf16[256,1536]{1,0:T(8,128)(2,1)} %get-tuple-element.980), channel_id=1, source_target_pairs={{16,0},{32,16},{48,32},{64,48},{80,64},{96,80},{112,96},{17,1},{33... | collective-permute-start | bytes 2359304 | tf_op jit(solution)/shard_map/while/body/eval_jaxpr/ppermute | solution.py:14
  787.1 15.3 %collective-permute-start = (bf16[256,1536]{1,0:T(8,128)(2,1)}, bf16[256,1536]{1,0:T(8,128)(2,1)S(1)}, u32[]{:S(2)}, u32[]{:S(2)}) collective-permute-start(bf16[256,1536]{1,0:T(8,128)(2,1)} %get-tuple-element.980), channel_id=1, source_target_pairs={{16,0},{32,16},{48,32},{64,48},{80,64},{96,80},{112,96},{17,1},{33... | collective-permute-start | bytes 2359304 | tf_op jit(solution)/shard_map/while/body/eval_jaxpr/ppermute | solution.py:14
  803.3 315.7 %collective-permute-start = (bf16[256,1536]{1,0:T(8,128)(2,1)}, bf16[256,1536]{1,0:T(8,128)(2,1)S(1)}, u32[]{:S(2)}, u32[]{:S(2)}) collective-permute-start(bf16[256,1536]{1,0:T(8,128)(2,1)} %get-tuple-element.980), channel_id=1, source_target_pairs={{16,0},{32,16},{48,32},{64,48},{80,64},{96,80},{112,96},{17,1},{33... | collective-permute-start | bytes 2359304 | tf_op jit(solution)/shard_map/while/body/eval_jaxpr/ppermute | solution.py:14
  1119.9 6.1 copy-start.14
  1151.5 6.2 copy-start.2
  1164.2 12.9 collective-permute-start
  1182.3 176.2 %reduce-scatter.4.cloned.1.call-start = ((), (), s32[]{:S(2)}) async-start(), calls=%async_computation.4 | async-start | bytes 7520256 | tf_op jit(solution)/shard_map/reduce_scatter | solution.py:214
  1192.5 266.1 %reduce-scatter.8.cloned.1.call-start = ((), (), s32[]{:S(2)}) async-start(), calls=%async_computation.6 | async-start | bytes 8355840 | tf_op jit(solution)/shard_map/reduce_scatter | solution.py:220
  (6 other events, 9.6 us)
Sparse Core Ops, SparseCore 0:
  10.5 51.8 all-gather.8
  64.9 66.1 all-gather.6
  133.5 68.4 all-gather.10
  520.7 168.3 all-reduce.1
  1182.5 78.7 reduce-scatter.5
  1266.0 92.5 reduce-scatter.3
  1362.8 95.7 reduce-scatter.7
where the time goes:
time: 1470 us
  waiting for transfers between devices  1150 us (78%)
  starting transfers between devices  158 us (11%)
  local copies, waits for them, and re-layouts  73.4 us (5%)
  matrix products  51.2 us (3%)
  other arithmetic  21.5 us (1%)
    ppermute x16, waiting for transfers between devices, passed_along(): return lax.ppermute(value, axis, pairs)  526 us
    psum x1, waiting for transfers between devices, shards(): lax.psum(term.astype(jnp.bfloat16), 'segment').astype(jnp.float32)  167 us
    ppermute x16, starting transfers between devices, passed_along(): return lax.ppermute(value, axis, pairs)  157 us
    reduce_scatter x1, waiting for transfers between devices, shards(): lax.psum_scatter(local_grads[2].astype(jnp.bfloat16), 'dp', scatter_dimen...  98.1 us
    reduce_scatter x1, waiting for transfers between devices, shards(): lax.psum_scatter(local_grads[0].astype(jnp.bfloat16), 'dp', scatter_dimen...  95.6 us
    all_gather x1, waiting for transfers between devices, shards(): lax.all_gather(w_hint[0], 'dp', axis=0, tiled=True)  71 us
    all_gather x1, waiting for transfers between devices, shards(): lax.all_gather(w_qkv[0], 'dp', axis=0, tiled=True)  68.6 us
    reduce_scatter x1, waiting for transfers between devices, shards(): lax.psum_scatter(local_grads[1].astype(jnp.bfloat16), 'dp', scatter_dimen...  68 us
  transfers between devices with their start and end apart: 23, of which 23 were waited for; matrix products, arithmetic and copies ran while one was open for 1% of the time, Pallas kernels for 0%

commit v1 on v0

v1 whole, which is shorter than its diff:
```python
import functools

import jax
import jax.numpy as jnp
from jax import lax
from jax.experimental import pallas as pl
from jax.experimental.pallas import tpu as pltpu
from jax.sharding import PartitionSpec as P

HEADS = 6
HEAD = 128
TILE = 64
ROWS = 256
WIDTH = 1536
HD = HEADS * HEAD
QKV = 3 * HD
CW = 256
CH = WIDTH // CW
SCALE = HEAD ** (-0.5)
MESH = pl.DeviceIdType.MESH
VMEM_LIMIT = 56 * 1024 * 1024
F32 = jnp.float32
BF16 = jnp.bfloat16


def dot(a, b, dims=((1,), (0,))):
    return lax.dot_general(a, b, (dims, ((), ())), preferred_element_type=F32)


def chain_place():
    z = lax.axis_index("z")
    core = lax.axis_index("core")
    section = z + 4 * core
    later = lax.rem(section + 1, 8)
    earlier = lax.rem(section + 7, 8)
    return (
        section,
        {"z": lax.rem(later, 4), "core": later // 4},
        {"z": lax.rem(earlier, 4), "core": earlier // 4},
    )


def greet(*others):
    barrier = pltpu.get_barrier_semaphore()
    for other in others:
        pl.semaphore_signal(barrier, inc=1, device_id=other, device_id_type=MESH)
    pl.semaphore_wait(barrier, len(others))


def head_probs(proj, bias, head):
    lo = head * HEAD
    queries = proj[:, lo : lo + HEAD]
    keys = proj[:, HD + lo : HD + lo + HEAD]
    scores = dot(queries, keys, ((1,), (1,))) * SCALE + bias
    shifted = jnp.exp(scores - jnp.max(scores, -1, keepdims=True))
    return shifted / jnp.sum(shifted, -1, keepdims=True)


def forward_chain(
    start_ref, bias_ref, wqkv_ref, wout_ref,
    control_ref, after_ref, proj_ref, att_ref,
    landed, leaving, acc, send_sem, recv_sem,
):
    section, later, earlier = chain_place()
    greet(later, earlier)

    @pl.when(section == 0)
    def _():
        for k in range(CH):
            landed[k] = start_ref[k]

    def hop(k):
        return pltpu.make_async_remote_copy(
            src_ref=leaving.at[k],
            dst_ref=landed.at[k],
            send_sem=send_sem.at[k],
            recv_sem=recv_sem.at[k],
            device_id=later,
            device_id_type=MESH,
        )

    squares = jnp.zeros((ROWS, 1), F32)
    for k in range(CH):
        @pl.when(section > 0)
        def _():
            hop(k).wait_recv()

        x = landed[k]
        wide = x.astype(F32)
        squares += jnp.sum(wide * wide, -1, keepdims=True)
        for n in range(3):
            cols = slice(n * HD, (n + 1) * HD)
            part = dot(x, wqkv_ref[k * CW : (k + 1) * CW, cols])
            if k == 0:
                acc[:, cols] = part
            elif k < CH - 1:
                acc[:, cols] += part
            else:
                inverse = lax.rsqrt(squares * (1.0 / WIDTH) + 1e-06)
                proj_ref[:, cols] = ((acc[:, cols] + part) * inverse).astype(BF16)
    bias = bias_ref[...]
    for h in range(HEADS):
        probs = head_probs(proj_ref, bias, h).astype(BF16)
        lo = 2 * HD + h * HEAD
        att_ref[:, h * HEAD : (h + 1) * HEAD] = dot(probs, proj_ref[:, lo : lo + HEAD]).astype(BF16)
    att = att_ref[...]
    for k in range(CH):
        out = landed[k].astype(F32) + dot(att, wout_ref[:, k * CW : (k + 1) * CW])
        leaving[k] = out.astype(BF16)

        @pl.when(section < 7)
        def _():
            hop(k).start()

    control_ref[...] = landed[...]
    after_ref[...] = leaving[...]

    @pl.when(section < 7)
    def _():
        for k in range(CH):
            hop(k).wait_send()


def backward_chain(
    hint_ref, control_ref, proj_ref, bias_ref, wqkv_ref, wout_ref,
    after_ref, gproj_ref,
    landed, leaving, probs_ref, acc, send_sem, recv_sem,
):
    section, later, earlier = chain_place()
    greet(later, earlier)
    bias = bias_ref[...]
    for h in range(HEADS):
        probs_ref[h] = head_probs(proj_ref, bias, h)
    squares = jnp.zeros((ROWS, 1), F32)
    for k in range(CH):
        wide = control_ref[k].astype(F32)
        squares += jnp.sum(wide * wide, -1, keepdims=True)
    inverse = lax.rsqrt(squares * (1.0 / WIDTH) + 1e-06)

    def hop(k):
        return pltpu.make_async_remote_copy(
            src_ref=leaving.at[k],
            dst_ref=landed.at[k],
            send_sem=send_sem.at[k],
            recv_sem=recv_sem.at[k],
            device_id=earlier,
            device_id_type=MESH,
        )

    @pl.when(section == 7)
    def _():
        for k in range(CH):
            landed[k] = jnp.zeros((ROWS, CW), BF16)

    for k in range(CH):
        @pl.when(section < 7)
        def _():
            hop(k).wait_recv()

        grad = (landed[k].astype(F32) + hint_ref[k]).astype(BF16)
        after_ref[k] = grad
        part = dot(grad, wout_ref[:, k * CW : (k + 1) * CW], ((1,), (1,)))
        if k == 0:
            acc[...] = part
        else:
            acc[...] += part
    through = jnp.zeros((ROWS, 1), F32)
    for h in range(HEADS):
        lo = h * HEAD
        grad_att = acc[:, lo : lo + HEAD].astype(BF16)
        queries = proj_ref[:, lo : lo + HEAD]
        keys = proj_ref[:, HD + lo : HD + lo + HEAD]
        values = proj_ref[:, 2 * HD + lo : 2 * HD + lo + HEAD]
        probs = probs_ref[h]
        grad_probs = dot(grad_att, values, ((1,), (1,)))
        grad_values = dot(probs.astype(BF16), grad_att, ((0,), (0,))).astype(BF16)
        total = jnp.sum(grad_probs * probs, -1, keepdims=True)
        grad_scores = (probs * (grad_probs - total) * SCALE).astype(BF16)
        grad_queries = dot(grad_scores, keys).astype(BF16)
        grad_keys = dot(grad_scores, queries, ((0,), (0,))).astype(BF16)
        for n, (grad, value) in enumerate(
            ((grad_queries, queries), (grad_keys, keys), (grad_values, values))
        ):
            gproj_ref[:, n * HD + lo : n * HD + lo + HEAD] = grad
            through += jnp.sum(grad.astype(F32) * value.astype(F32), -1, keepdims=True)
    slope = inverse * inverse * through * (1.0 / WIDTH)
    grad_proj = gproj_ref[...]
    for k in range(CH):
        grad_normed = dot(grad_proj, wqkv_ref[k * CW : (k + 1) * CW, :], ((1,), (1,)))
        out = after_ref[k].astype(F32) + inverse * grad_normed - control_ref[k].astype(F32) * slope
        leaving[k] = out.astype(BF16)

        @pl.when(section > 0)
        def _():
            hop(k).start()

    @pl.when(section > 0)
    def _():
        for k in range(CH):
            hop(k).wait_send()


def vmem_call(kernel, out_shape, scratch, collective_id, flops):
    spec = pl.BlockSpec(memory_space=pltpu.VMEM)
    return lambda *args: pl.pallas_call(
        kernel,
        out_shape=out_shape,
        in_specs=[spec] * len(args),
        out_specs=[spec] * len(out_shape),
        scratch_shapes=scratch,
        compiler_params=pltpu.CompilerParams(
            collective_id=collective_id, has_side_effects=True, vmem_limit_bytes=VMEM_LIMIT
        ),
        cost_estimate=pl.CostEstimate(flops=flops, bytes_accessed=12_000_000, transcendentals=0),
    )(*args)


def chunked(value):
    return value.reshape(ROWS, CH, CW).transpose(1, 0, 2)


def flat(value):
    return value.transpose(1, 0, 2).reshape(ROWS, WIDTH)


def swap_roles(value):
    return lax.ppermute(value, ("xlo", "core"), [(0, 0), (1, 2), (2, 1), (3, 3)])


def of_clip(value):
    other = lax.ppermute(value, "core", [(0, 1), (1, 0)])
    return jnp.where(lax.axis_index("core") == lax.axis_index("xlo"), value, other)


def mask_bias(offset, mask, layout):
    row_tile = jnp.arange(4)[:, None]
    col_tile = jnp.arange(4)[None, :]
    near_window = jnp.abs(col_tile - row_tile - offset[:, None]) <= 1
    permitted = (row_tile == col_tile) | near_window & (mask == 1)
    holds = layout[None, :] == jnp.arange(ROWS)[:, None]
    tile_of = jnp.sum(jnp.where(holds, jnp.arange(ROWS)[None, :] // TILE, 0), 1)
    member = (tile_of[:, None] == jnp.arange(4)[None, :]).astype(BF16)
    allowed = dot(dot(member, permitted.astype(BF16)).astype(BF16), member, ((1,), (1,)))
    return jnp.where(allowed > 0.5, 0.0, -1e30)


def shards(
    control_in, base_in, base_update, out_gain, cotangent,
    w_qkv, w_out, w_hint, window_offset, tile_mask, token_layout,
):
    plane = ("xhi", "y", "xlo")
    small = jnp.concatenate([window_offset.reshape(-1), tile_mask.reshape(-1)])
    small = swap_roles(small)
    layout = of_clip(token_layout[0])
    bias = mask_bias(small[:4], small[4:].reshape(4, 4), layout)
    control = of_clip(control_in)
    base = of_clip(base_in)
    cot = of_clip(cotangent)
    update = swap_roles(base_update[0])
    weight_qkv = lax.all_gather(swap_roles(w_qkv[0]), plane, axis=0, tiled=True)
    weight_out = lax.all_gather(swap_roles(w_out[0]), plane, axis=0, tiled=True)
    weight_hint = lax.all_gather(swap_roles(w_hint[0]), plane, axis=0, tiled=True)

    chunk_shape = jax.ShapeDtypeStruct((CH, ROWS, CW), BF16)
    control_s, control_next, proj, att = vmem_call(
        forward_chain,
        [
            chunk_shape,
            chunk_shape,
            jax.ShapeDtypeStruct((ROWS, QKV), BF16),
            jax.ShapeDtypeStruct((ROWS, HD), BF16),
        ],
        [
            pltpu.VMEM((CH, ROWS, CW), BF16),
            pltpu.VMEM((CH, ROWS, CW), BF16),
            pltpu.VMEM((ROWS, QKV), F32),
            pltpu.SemaphoreType.DMA((CH,)),
            pltpu.SemaphoreType.DMA((CH,)),
        ],
        1,
        40_000_000_000,
    )(chunked(control), bias, weight_qkv, weight_out)

    after = flat(control_next)
    term = dot(after, weight_hint) + update.astype(F32)
    summed = base.astype(F32) + lax.psum(term.astype(BF16), ("z", "core")).astype(F32)

    inverse = lax.rsqrt(jnp.mean(summed * summed, -1, keepdims=True) + 1e-06)
    grad_normed = cot.astype(F32) * out_gain
    grad_summed = (
        inverse * grad_normed
        - summed * inverse**3 * jnp.mean(grad_normed * summed, -1, keepdims=True)
    ).astype(BF16)

    mine = swap_roles(summed.astype(BF16)).astype(F32)
    features = mine * lax.rsqrt(jnp.mean(mine * mine, -1, keepdims=True) + 1e-06) * out_gain

    hint_grad = dot(grad_summed, weight_hint, ((1,), (1,)))
    grad_hint = dot(after, grad_summed, ((0,), (0,))).astype(BF16)
    sum_hint = lax.psum_scatter(grad_hint, plane, scatter_dimension=0, tiled=True)

    grad_after, grad_proj = vmem_call(
        backward_chain,
        [chunk_shape, jax.ShapeDtypeStruct((ROWS, QKV), BF16)],
        [
            pltpu.VMEM((CH, ROWS, CW), BF16),
            pltpu.VMEM((CH, ROWS, CW), BF16),
            pltpu.VMEM((HEADS, ROWS, ROWS), F32),
            pltpu.VMEM((ROWS, HD), F32),
            pltpu.SemaphoreType.DMA((CH,)),
            pltpu.SemaphoreType.DMA((CH,)),
        ],
        2,
        40_000_000_000,
    )(chunked(hint_grad), control_s, proj, bias, weight_qkv, weight_out)

    wide = flat(control_s).astype(F32)
    normed = (wide * lax.rsqrt(jnp.mean(wide * wide, -1, keepdims=True) + 1e-06)).astype(BF16)
    grad_qkv = dot(normed, grad_proj, ((0,), (0,))).astype(BF16)
    grad_out = dot(att, flat(grad_after), ((0,), (0,))).astype(BF16)
    sum_qkv = lax.psum_scatter(grad_qkv, plane, scatter_dimension=0, tiled=True)
    sum_out = lax.psum_scatter(grad_out, plane, scatter_dimension=0, tiled=True)
    factor = 4096.0 ** (-0.5)
    return (
        features,
        (swap_roles(sum_qkv).astype(F32) * factor)[None],
        (swap_roles(sum_out).astype(F32) * factor)[None],
        (swap_roles(sum_hint).astype(F32) * factor)[None],
    )


def solution(mesh):
    parts = jax.sharding.Mesh(
        mesh.devices.reshape(2, 4, 2, 4, 2), ("xlo", "z", "xhi", "y", "core")
    )
    segment = ("xlo", "z")
    dp = ("xhi", "y", "core")
    by_rows = P(dp, None)
    by_both = P(segment, dp, None)
    placed = (
        by_rows, by_rows, by_both, P(), by_rows, by_both, by_both, by_both,
        P(segment, None), P(segment, None, None), by_rows,
    )
    return jax.shard_map(
        shards,
        mesh=parts,
        in_specs=placed,
        out_specs=(by_rows, by_both, by_both, by_both),
        check_vma=False,
    )
```

time: 1470 us -> 1050 us (0.71)
  waiting for transfers between devices: 1150 us -> 745 us
  Pallas kernels: 0 us -> 138 us
  starting transfers between devices: 158 us -> 96.2 us
  local copies, waits for them, and re-layouts: 73.4 us -> 16.3 us
  matrix products: 51.2 us -> 22.7 us
    ppermute x16 -> x13, waiting for transfers between devices: 526 us -> 71.8 us  [the longest x9 71.8 us: swap_roles(): lax.ppermute(value, ('xlo', 'core'), [(0, 0), (1, 2), (2, 1), (3, 3)])]
    pallas_call x0 -> x2, Pallas kernels: none -> 138 us  [vmem_call(): pl.pallas_call(kernel, out_shape=out_shape, in_specs=[spec] * len(args),...]
    psum x1, waiting for transfers between devices: 167 us -> 62.5 us  [shards(): lax.psum(term.astype(BF16), ('z', 'core')).astype(F32)]
    all_gather x3, waiting for transfers between devices: 192 us -> 281 us  [the longest x1 158 us: shards(): weight_qkv = lax.all_gather(swap_roles(w_qkv[0]), plane, axis=0, tiled=True)]
    reduce_scatter x3, waiting for transfers between devices: 262 us -> 330 us  [the longest x1 169 us: shards(): lax.psum_scatter(grad_hint, plane, scatter_dimension=0, tiled=True)]
    ppermute x16 -> x13, starting transfers between devices: 157 us -> 95.5 us  [the longest x9 87.1 us: swap_roles(): lax.ppermute(value, ('xlo', 'core'), [(0, 0), (1, 2), (2, 1), (3, 3)])]
    dot_general x14 -> x6, matrix products: 49.4 us -> 22.7 us  [dot(): return lax.dot_general(a, b, (dims, ((), ())), preferred_element_type=F32)]
    while x11 -> x0, local copies, waits for them, and re-layouts: 23.2 us -> none  [the longest x3 15.8 us: shards(): local_grads = lax.fori_loop(0, segments, backward_turn, start_back)[1]]
  transfers between devices with their start and end apart: 23 -> 20, of which waited for: 23 -> 12; matrix products, arithmetic and copies ran while one was open for 1% -> 3% of each run, Pallas kernels for 0% -> 7%
where the time goes in v1:
time: 1050 us
  waiting for transfers between devices  745 us (71%)
  Pallas kernels  138 us (13%)
  starting transfers between devices  96.2 us (9%)
  matrix products  22.7 us (2%)
  local copies, waits for them, and re-layouts  16.3 us (2%)
  other arithmetic  15 us (1%)
  between operations  14.4 us (1%)
    reduce_scatter x1, waiting for transfers between devices, shards(): lax.psum_scatter(grad_hint, plane, scatter_dimension=0, tiled=True)  169 us
    all_gather x1, waiting for transfers between devices, shards(): weight_qkv = lax.all_gather(swap_roles(w_qkv[0]), plane, axis=0, tiled=True)  158 us
    reduce_scatter x1, waiting for transfers between devices, shards(): sum_qkv = lax.psum_scatter(grad_qkv, plane, scatter_dimension=0, tiled=True)  151 us
    pallas_call x2, Pallas kernels, vmem_call(): pl.pallas_call(kernel, out_shape=out_shape, in_specs=[spec] * len(args),...  138 us
    all_gather x1, waiting for transfers between devices, shards(): lax.all_gather(swap_roles(w_hint[0]), plane, axis=0, tiled=True)  96.3 us
    ppermute x9, starting transfers between devices, swap_roles(): lax.ppermute(value, ('xlo', 'core'), [(0, 0), (1, 2), (2, 1), (3, 3)])  87.1 us
    ppermute x9, waiting for transfers between devices, swap_roles(): lax.ppermute(value, ('xlo', 'core'), [(0, 0), (1, 2), (2, 1), (3, 3)])  71.8 us
    psum x1, waiting for transfers between devices, shards(): lax.psum(term.astype(BF16), ('z', 'core')).astype(F32)  62.5 us
  transfers between devices with their start and end apart: 20, of which 12 were waited for; matrix products, arithmetic and copies ran while one was open for 3% of the time, Pallas kernels for 7%

profile of v1, /device:TPU:1, one launch (start us, length us, event | category | flops | bytes accessed | tf_op | source)
XLA Modules:
  0.0 1047.2 jit_solution(16457401939763319083)
XLA Ops:
  7.2 4.6 collective-permute-start.5
  11.9 3.0 collective-permute-done.5
  15.6 3.6 collective-permute-start.4
  19.3 6.2 collective-permute-done.4
  26.3 3.6 collective-permute-start.6
  30.0 15.6 %collective-permute-done.6 = bf16[96,2560]{1,0:T(8,128)(2,1)S(1)} collective-permute-done((bf16[96,2560]{1,0:T(8,128)(2,1)}, bf16[96,2560]{1,0:T(8,128)(2,1)S(1)}, u32[]{:S(2)}, u32[]{:S(2)}) %collective-permute-start.6) | collective-permute-done | bytes 491552 | tf_op jit(solution)/shard_map/ppermute | solution.py:227
  50.3 3.6 collective-permute-start.7
  54.0 8.1 collective-permute-start.9
  63.7 2.1 broadcast_select_fusion.2
  65.9 2.3 copy.25
  68.1 26.2 %all-gather.6.cloned.1.call-done.wout_ref = bf16[768,1536]{1,0:T(8,128)(2,1)} async-done(((bf16[48,1536]{1,0:T(8,128)(2,1)}), bf16[768,1536]{1,0:T(8,128)(2,1)}) %all-gather.6.cloned.1.call-update) | async-done | bytes 2359312 | tf_op jit(solution)/shard_map/all_gather | solution.py:261
  94.3 158.3 %all-gather.4.cloned.1.call-done.wqkv_ref = bf16[1536,2304]{1,0:T(8,128)(2,1)} async-done(((bf16[96,2304]{1,0:T(8,128)(2,1)}), bf16[1536,2304]{1,0:T(8,128)(2,1)}) %all-gather.4.cloned.1.call-update) | async-done | bytes 7077904 | tf_op jit(solution)/shard_map/all_gather | solution.py:260
  252.7 74.9 %shard_map.138 = (bf16[6,256,256]{2,1,0:T(8,128)(2,1)}, bf16[6,256,256]{2,1,0:T(8,128)(2,1)}, bf16[256,2304]{1,0:T(8,128)(2,1)}, bf16[256,768]{1,0:T(8,128)(2,1)}) custom-call(bf16[6,256,256]{2,1,0:T(8,128)(2,1)} %bitcast.45, f32[256,256]{1,0:T(8,128)} %fusion.6.bias_ref, bf16[1536,2304]{1,0:T(8,128)(2,1)} %all-gather.4.cloned.1.call-done.wqkv_ref, ...), custom_call_target="tpu_custom_call" | custom-call | flops 40000000000 | bytes 12000000 | tf_op jit(solution)/shard_map/pallas_call | solution.py:205
  329.0 96.3 %all-gather.8.cloned.1.call-done = bf16[1536,2560]{1,0:T(8,128)(2,1)} async-done(((bf16[96,2560]{1,0:T(8,128)(2,1)}), bf16[1536,2560]{1,0:T(8,128)(2,1)}) %all-gather.8.cloned.1.call-update) | async-done | bytes 7864336 | tf_op jit(solution)/shard_map/all_gather | solution.py:262
  425.3 6.8 fusion
  432.4 62.5 %all-reduce.2.cloned.1.call-done = bf16[256,2560]{1,0:T(8,128)(2,1)} async-done(((bf16[256,2560]{1,0:T(8,128)(2,1)}), bf16[256,2560]{1,0:T(8,128)(2,1)}) %all-reduce.2.cloned.1.call-update) | async-done | bytes 1310736 | tf_op jit(solution)/shard_map/psum | solution.py:286
  494.9 3.2 multiply_reduce_fusion.1
  498.1 2.1 subtract_convert_fusion
  500.2 2.2 fusion.19
  504.1 62.9 %shard_map.139 = (bf16[6,256,256]{2,1,0:T(8,128)(2,1)}, bf16[256,2304]{1,0:T(8,128)(2,1)}) custom-call(f32[6,256,256]{2,1,0:T(8,128)} %bitcast.43, bf16[6,256,256]{2,1,0:T(8,128)(2,1)} %get-tuple-element.11.control_ref, bf16[256,2304]{1,0:T(8,128)(2,1)} %get-tuple-element.12.proj_ref, f32[256,256]{1,0:T(8,128)} %fusion.6.bias_ref, ...), custom_call_target="tpu_custom_call" | custom-call | flops 40000000000 | bytes 12000000 | tf_op jit(solution)/shard_map/pallas_call | solution.py:205
  568.4 2.2 convolution_convert_fusion.2
  576.3 4.9 convolution_convert_fusion.1
  582.6 5.3 convolution_convert_fusion
  589.1 53.8 %collective-permute-start.8 = (bf16[256,2560]{1,0:T(8,128)(2,1)S(1)}, bf16[256,2560]{1,0:T(8,128)(2,1)S(1)}, u32[]{:S(2)}, u32[]{:S(2)}) collective-permute-start(bf16[256,2560]{1,0:T(8,128)(2,1)S(1)} %copy-done.5), channel_id=1, source_target_pairs={{0,0},{1,64},{64,1},{65,65},{2,2},{3,66},{66,3},{67,67},{4,4},{5,6... | collective-permute-start | bytes 3932168 | tf_op jit(solution)/shard_map/ppermute | solution.py:227
  643.0 41.2 %collective-permute-done.8 = bf16[256,2560]{1,0:T(8,128)(2,1)S(1)} collective-permute-done((bf16[256,2560]{1,0:T(8,128)(2,1)S(1)}, bf16[256,2560]{1,0:T(8,128)(2,1)S(1)}, u32[]{:S(2)}, u32[]{:S(2)}) %collective-permute-start.8) | collective-permute-done | bytes 1310752 | tf_op jit(solution)/shard_map/ppermute | solution.py:227
  684.5 9.7 reduce-scatter.6.cloned.1.call-done
  694.2 8.7 collective-permute-start.11
  704.7 151.2 %reduce-scatter.4.cloned.1.call-done = bf16[96,2304]{1,0:T(8,128)(2,1)} async-done(((bf16[1536,2304]{1,0:T(8,128)(2,1)}), bf16[96,2304]{1,0:T(8,128)(2,1)}) %reduce-scatter.4.cloned.1.call-update) | async-done | bytes 442384 | tf_op jit(solution)/shard_map/reduce_scatter | solution.py:321
  855.9 3.6 collective-permute-start.10
  860.2 168.8 %reduce-scatter.8.cloned.1.call-done = bf16[96,2560]{1,0:T(8,128)(2,1)} async-done(((bf16[1536,2560]{1,0:T(8,128)(2,1)}), bf16[96,2560]{1,0:T(8,128)(2,1)}) %reduce-scatter.8.cloned.1.call-update) | async-done | bytes 491536 | tf_op jit(solution)/shard_map/reduce_scatter | solution.py:300
  1029.0 3.6 collective-permute-start.12
  1033.6 5.8 collective-permute-done.12
  (83 shorter events, 25.8 us)
Async XLA Ops:
  7.2 42.8 %copy-start.7 = (bf16[256,1536]{1,0:T(8,128)(2,1)S(1)}, bf16[256,1536]{1,0:T(8,128)(2,1)}, u32[]{:S(2)}) copy-start(bf16[256,1536]{1,0:T(8,128)(2,1)} %param.11) | copy-start | bytes 2359300
  7.2 46.8 %copy-start = (bf16[256,2560]{1,0:T(8,128)(2,1)S(1)}, bf16[256,2560]{1,0:T(8,128)(2,1)}, u32[]{:S(2)}) copy-start(bf16[256,2560]{1,0:T(8,128)(2,1)} %param.15) | copy-start | bytes 3932164
  7.2 87.2 %all-gather.6.cloned.1.call-start = ((), (), s32[]{:S(2)}) async-start(), calls=%async_computation.4 | async-start | bytes 2506752 | tf_op jit(solution)/shard_map/all_gather | solution.py:261
  7.2 7.7 collective-permute-start.5
  15.6 46.8 %copy-start.13 = (s32[1,256]{1,0:T(1,128)S(1)}, s32[1,256]{1,0:T(1,128)}, u32[]{:S(2)}) copy-start(s32[1,256]{1,0:T(1,128)} %param.21) | copy-start | bytes 3076
  15.6 237.1 %all-gather.4.cloned.1.call-start = ((), (), s32[]{:S(2)}) async-start(), calls=%async_computation.3 | async-start | bytes 7520256 | tf_op jit(solution)/shard_map/all_gather | solution.py:260
  15.6 9.8 collective-permute-start.4
  26.3 399.0 %all-gather.8.cloned.1.call-start = ((), (), s32[]{:S(2)}) async-start(), calls=%async_computation.5 | async-start | bytes 8355840 | tf_op jit(solution)/shard_map/all_gather | solution.py:262
  26.3 19.3 %collective-permute-start.6 = (bf16[96,2560]{1,0:T(8,128)(2,1)}, bf16[96,2560]{1,0:T(8,128)(2,1)S(1)}, u32[]{:S(2)}, u32[]{:S(2)}) collective-permute-start(bf16[96,2560]{1,0:T(8,128)(2,1)} %bitcast.51), channel_id=1, source_target_pairs={{0,0},{1,64},{64,1},{65,65},{2,2},{3,66},{66,3},{67,67},{4,4},{5,6... | collective-permute-start | bytes 1474568 | tf_op jit(solution)/shard_map/ppermute | solution.py:227
  46.4 448.4 %all-reduce.2.cloned.1.call-start = ((), (), s32[]{:S(2)}) async-start(), calls=%async_computation.6 | async-start | bytes 2621440 | tf_op jit(solution)/shard_map/psum | solution.py:286
  46.5 15.9 %collective-permute-start.2 = (s32[256]{0:T(256)}, s32[256]{0:T(256)S(1)}, u32[]{:S(2)}, u32[]{:S(2)}) collective-permute-start(s32[256]{0:T(256)} %bitcast.48), channel_id=1, source_target_pairs={{0,1},{1,0},{2,3},{3,2},{4,5},{5,4},{6,7},{7,6},{8,9},{9,8},{10,11... | collective-permute-start | bytes 3080 | tf_op jit(solution)/shard_map/ppermute | solution.py:231
  48.0 14.1 %collective-permute-start.3 = (s32[20]{0:T(128)S(1)}, s32[20]{0:T(128)S(1)}, u32[]{:S(2)}, u32[]{:S(2)}) collective-permute-start(s32[20]{0:T(128)S(1)} %pad_add_fusion), channel_id=1, source_target_pairs={{0,0},{1,64},{64,1},{65,65},{2,2},{3,66},{66,3},{67,67},{4,4},{5,6... | collective-permute-start | bytes 248 | tf_op jit(solution)/shard_map/ppermute | solution.py:227
  50.3 13.5 %collective-permute-start.1 = (bf16[256,1536]{0,1:T(8,128)(2,1)S(1)}, bf16[256,1536]{0,1:T(8,128)(2,1)}, u32[]{:S(2)}, u32[]{:S(2)}) collective-permute-start(bf16[256,1536]{0,1:T(8,128)(2,1)S(1)} %copy.24), channel_id=1, source_target_pairs={{0,1},{1,0},{2,3},{3,2},{4,5},{5,4},{6,7},{7,6},{8,9},{9,8},{10,11... | collective-permute-start | bytes 2359304 | tf_op jit(solution)/shard_map/ppermute | solution.py:231
  50.3 278.6 %collective-permute-start.7 = (bf16[256,2560]{1,0:T(8,128)(2,1)}, bf16[256,2560]{1,0:T(8,128)(2,1)}, u32[]{:S(2)}, u32[]{:S(2)}) collective-permute-start(bf16[256,2560]{1,0:T(8,128)(2,1)} %bitcast.50), channel_id=1, source_target_pairs={{0,0},{1,64},{64,1},{65,65},{2,2},{3,66},{66,3},{67,67},{4,4},{5,6... | collective-permute-start | bytes 3932168 | tf_op jit(solution)/shard_map/ppermute | solution.py:227
  54.0 378.4 %collective-permute-start.9 = (bf16[256,2560]{1,0:T(8,128)(2,1)S(1)}, bf16[256,2560]{1,0:T(8,128)(2,1)S(1)}, u32[]{:S(2)}, u32[]{:S(2)}) collective-permute-start(bf16[256,2560]{1,0:T(8,128)(2,1)S(1)} %copy-done), channel_id=1, source_target_pairs={{0,1},{1,0},{2,3},{3,2},{4,5},{5,4},{6,7},{7,6},{8,9},{9,8},{10,11... | collective-permute-start | bytes 3932168 | tf_op jit(solution)/shard_map/ppermute | solution.py:231
  62.1 370.3 %collective-permute-start = (bf16[256,2560]{1,0:T(8,128)(2,1)}, bf16[256,2560]{1,0:T(8,128)(2,1)}, u32[]{:S(2)}, u32[]{:S(2)}) collective-permute-start(bf16[256,2560]{1,0:T(8,128)(2,1)} %param.12), channel_id=1, source_target_pairs={{0,1},{1,0},{2,3},{3,2},{4,5},{5,4},{6,7},{7,6},{8,9},{9,8},{10,11... | collective-permute-start | bytes 3932168 | tf_op jit(solution)/shard_map/ppermute | solution.py:231
  425.3 69.6 %copy-start.12 = (f32[2560]{0:T(1024)S(1)}, f32[2560]{0:T(1024)}, u32[]{:S(2)}) copy-start(f32[2560]{0:T(1024)} %param.14) | copy-start | bytes 30724
  432.2 262.0 %reduce-scatter.6.cloned.1.call-start = ((), (), s32[]{:S(2)}) async-start(), calls=%async_computation.8 | async-start | bytes 2506752 | tf_op jit(solution)/shard_map/reduce_scatter | solution.py:322
  494.9 3.2 copy-start.3
  494.9 5.3 slice-start
  498.0 2.2 slice-start.1
  500.2 2.3 copy-start.1
  567.0 1.5 copy-start.10
  570.7 285.2 %reduce-scatter.4.cloned.1.call-start = ((), (), s32[]{:S(2)}) async-start(), calls=%async_computation.7 | async-start | bytes 7520256 | tf_op jit(solution)/shard_map/reduce_scatter | solution.py:321
  575.0 1.3 copy-start.6
  581.2 1.3 copy-start.2
  581.3 447.7 %reduce-scatter.8.cloned.1.call-start = ((), (), s32[]{:S(2)}) async-start(), calls=%async_computation.9 | async-start | bytes 8355840 | tf_op jit(solution)/shard_map/reduce_scatter | solution.py:300
  587.8 1.3 copy-start.5
  589.1 95.0 %collective-permute-start.8 = (bf16[256,2560]{1,0:T(8,128)(2,1)S(1)}, bf16[256,2560]{1,0:T(8,128)(2,1)S(1)}, u32[]{:S(2)}, u32[]{:S(2)}) collective-permute-start(bf16[256,2560]{1,0:T(8,128)(2,1)S(1)} %copy-done.5), channel_id=1, source_target_pairs={{0,0},{1,64},{64,1},{65,65},{2,2},{3,66},{66,3},{67,67},{4,4},{5,6... | collective-permute-start | bytes 3932168 | tf_op jit(solution)/shard_map/ppermute | solution.py:227
  694.2 165.3 %collective-permute-start.11 = (bf16[48,1536]{1,0:T(8,128)(2,1)}, bf16[48,1536]{1,0:T(8,128)(2,1)S(1)}, u32[]{:S(2)}, u32[]{:S(2)}) collective-permute-start(bf16[48,1536]{1,0:T(8,128)(2,1)} %reduce-scatter.6.cloned.1.call-done), channel_id=1, source_target_pairs={{0,0},{1,64},{64,1},{65,65},{2,2},{3,66},{66,3},{67,67},{4,4},{5,6... | collective-permute-start | bytes 442376 | tf_op jit(solution)/shard_map/ppermute | solution.py:227
  855.9 176.7 %collective-permute-start.10 = (bf16[96,2304]{1,0:T(8,128)(2,1)}, bf16[96,2304]{1,0:T(8,128)(2,1)S(1)}, u32[]{:S(2)}, u32[]{:S(2)}) collective-permute-start(bf16[96,2304]{1,0:T(8,128)(2,1)} %reduce-scatter.4.cloned.1.call-done), channel_id=1, source_target_pairs={{0,0},{1,64},{64,1},{65,65},{2,2},{3,66},{66,3},{67,67},{4,4},{5,6... | collective-permute-start | bytes 1327112 | tf_op jit(solution)/shard_map/ppermute | solution.py:227
  1029.0 10.3 collective-permute-start.12
  (4 other events, 3.3 us)
Sparse Core Ops, SparseCore 0:
  15.7 78.5 all-gather.5
  96.0 156.6 all-gather.3
  254.9 170.3 all-gather.7
  432.3 62.5 all-reduce.1
  570.8 123.3 reduce-scatter.5
  696.5 159.3 reduce-scatter.3
  858.4 170.5 reduce-scatter.7

commit v2 on v1

v2 whole, which is shorter than its diff:
```python
import functools

import jax
import jax.numpy as jnp
from jax import lax
from jax.experimental import pallas as pl
from jax.experimental.pallas import tpu as pltpu
from jax.sharding import PartitionSpec as P

HEADS = 6
HEAD = 128
TILE = 64
ROWS = 256
WIDTH = 1536
FEAT = 2560
HD = HEADS * HEAD
QKV = 3 * HD
CW = 256
CH = WIDTH // CW
SCALE = HEAD ** (-0.5)
MESH = pl.DeviceIdType.MESH
VMEM_LIMIT = 60 * 1024 * 1024
F32 = jnp.float32
BF16 = jnp.bfloat16
QKV_CUT = (96, ((0, 640, 1152), (1152, 1792, 2304)))
OUT_CUT = (48, ((0, 384, 768), (768, 1152, 1536)))
HINT_CUT = (96, ((0, 640, 1280), (1280, 1920, 2560)))


def dot(a, b, dims=((1,), (0,))):
    return lax.dot_general(a, b, (dims, ((), ())), preferred_element_type=F32)


class Place:
    def __init__(self):
        self.xlo, self.z, self.xhi, self.y, self.core = (
            lax.axis_index(name) for name in ("xlo", "z", "xhi", "y", "core")
        )
        self.x = 2 * self.xhi + self.xlo
        self.section = self.z + 4 * self.core
        later = lax.rem(self.section + 1, 8)
        earlier = lax.rem(self.section + 7, 8)
        self.later = {"z": lax.rem(later, 4), "core": later // 4}
        self.earlier = {"z": lax.rem(earlier, 4), "core": earlier // 4}
        self.sibling = {"core": 1 - self.core}
        self.partner = {"xlo": 1 - self.xlo, "core": 1 - self.core}
        self.moved = self.xlo != self.core

    def along_x(self, by):
        x = lax.rem(self.x + by, 4)
        return {"xhi": x // 2, "xlo": lax.rem(x, 2)}

    def along_y(self, by):
        return {"y": lax.rem(self.y + by, 4)}

    def neighbour(self, half, ring, by):
        return self.along_y(by) if half == ring else self.along_x(by)

    def block(self, half, first, second):
        dx, dy = (second, first) if half == 0 else (first, second)
        x = lax.rem(self.x + dx, 4)
        y = lax.rem(self.y + dy, 4)
        return (x // 2) * 8 + y * 2 + lax.rem(x, 2)

    def greet(self):
        others = (
            self.later, self.earlier, self.sibling, self.partner,
            self.along_x(1), self.along_x(3), self.along_y(1), self.along_y(3),
        )
        barrier = pltpu.get_barrier_semaphore()
        for other in others:
            pl.semaphore_signal(barrier, inc=1, device_id=other, device_id_type=MESH)
        pl.semaphore_wait(barrier, len(others))


def remote(src, dst, send_sem, recv_sem, to):
    return pltpu.make_async_remote_copy(
        src_ref=src, dst_ref=dst, send_sem=send_sem, recv_sem=recv_sem,
        device_id=to, device_id_type=MESH,
    )


def rows_of(index, rows):
    return pl.ds(pl.multiple_of(index * rows, rows), rows)


class Gather:
    def __init__(self, place, shard, full, cut, send_sem, recv_sem, own_sem):
        self.place, self.shard, self.full = place, shard, full
        self.rows, self.cuts = cut
        self.send_sem, self.recv_sem, self.own_sem = send_sem, recv_sem, own_sem

    def region(self, half, first, second, part):
        lo, mid, hi = self.cuts[half]
        lo, hi = ((lo, hi), (lo, mid), (mid, hi))[part]
        index = self.place.block(half, first, second)
        return self.full.at[rows_of(index, self.rows), lo:hi]

    def copy(self, half, slot, first, second, part, ring=0, by=1):
        ref = self.region(half, first, second, part)
        return remote(
            ref, ref, self.send_sem.at[half, slot], self.recv_sem.at[half, slot],
            self.place.neighbour(half, ring, by),
        )

    def own(self, half):
        lo, _, hi = self.cuts[half]
        return self.shard.at[:, lo:hi], self.region(half, 0, 0, 0)

    def moved_own(self, half, index=None):
        src, dst = self.own(half)
        if index is not None:
            lo, _, hi = self.cuts[half]
            dst = self.full.at[rows_of(index, self.rows), lo:hi]
        return remote(
            src, dst, self.send_sem.at[half, 20], self.recv_sem.at[half, 20], self.place.partner
        )

    def kept_own(self, half):
        src, dst = self.own(half)
        return pltpu.make_async_copy(src, dst, self.own_sem.at[half])

    def sends(self, half):
        yield 0, (0, 0), 0, 0, 1
        yield 1, (0, 0), 0, 0, 3
        yield 2, (3, 0), 1, 0, 1
        yield 3, (1, 0), 2, 0, 3
        for j, first in enumerate((0, 3, 1, 2)):
            yield 4 + 4 * j, (first, 0), 0, 1, 1
            yield 5 + 4 * j, (first, 0), 0, 1, 3
            yield 6 + 4 * j, (first, 3), 1, 1, 1
            yield 7 + 4 * j, (first, 1), 2, 1, 3

    def send(self, half, *slots):
        plan = {entry[0]: entry for entry in self.sends(half)}
        for slot in slots:
            _, block, part, ring, by = plan[slot]
            self.copy(half, slot, *block, part, ring, by).start()

    def wait(self, half, *slots):
        plan = {0: (3, 0, 0), 1: (1, 0, 0), 2: (2, 0, 1), 3: (2, 0, 2)}
        for j, first in enumerate((0, 3, 1, 2)):
            plan |= {
                4 + 4 * j: (first, 3, 0), 5 + 4 * j: (first, 1, 0),
                6 + 4 * j: (first, 2, 1), 7 + 4 * j: (first, 2, 2),
            }
        for slot in slots:
            self.copy(half, slot, *plan[slot]).wait_recv()

    def start_own(self, half):
        place = self.place

        @pl.when(place.moved)
        def _():
            self.moved_own(half, place.xhi * 8 + place.y * 2 + 1 - place.xlo).start()

        @pl.when(jnp.logical_not(place.moved))
        def _():
            self.kept_own(half).start()

    def wait_own(self, half):
        @pl.when(self.place.moved)
        def _():
            self.moved_own(half).wait_recv()

        @pl.when(jnp.logical_not(self.place.moved))
        def _():
            self.kept_own(half).wait()

    def wait_sent(self):
        for half in range(2):
            for slot, block, part, ring, by in self.sends(half):
                self.copy(half, slot, *block, part, ring, by).wait_send()

            @pl.when(self.place.moved)
            def _():
                self.moved_own(half).wait_send()


def start_own(parts):
    for part in parts:
        for half in range(2):
            part.start_own(half)


def gather(parts):
    pairs = [(part, half) for part in parts for half in range(2)]
    for part, half in pairs:
        part.wait_own(half)
        part.send(half, 0, 1, 4, 5)
    for part, half in pairs:
        part.wait(half, 0)
        part.send(half, 2, 8, 9)
        part.wait(half, 1)
        part.send(half, 3, 12, 13)
    for part, half in pairs:
        part.wait(half, 4)
        part.send(half, 6)
        part.wait(half, 5)
        part.send(half, 7)
    for part, half in pairs:
        part.wait(half, 2, 3)
        part.send(half, 16, 17)
    for j in (1, 2, 3):
        for part, half in pairs:
            part.wait(half, 4 + 4 * j)
            part.send(half, 6 + 4 * j)
            part.wait(half, 5 + 4 * j)
            part.send(half, 7 + 4 * j)
    for part, half in pairs:
        for j in range(4):
            part.wait(half, 6 + 4 * j, 7 + 4 * j)


class Reduce:
    def __init__(self, place, grad, landing, total, result, cut, send_sem, recv_sem):
        self.place, self.grad, self.landing = place, grad, landing
        self.total, self.result = total, result
        self.rows, self.cuts = cut
        self.send_sem, self.recv_sem = send_sem, recv_sem

    def columns(self, half, part):
        lo, mid, hi = self.cuts[half]
        return ((lo, hi), (lo, mid), (mid, hi))[part]

    def region(self, half, first, second, part):
        lo, hi = self.columns(half, part)
        return self.grad.at[rows_of(self.place.block(half, first, second), self.rows), lo:hi]

    def slot_ref(self, half, slot, part):
        base = self.cuts[half][0]
        lo, hi = self.columns(half, part)
        return self.landing.at[half, slot, :, lo - base : hi - base]

    def copy(self, half, sem, first, second, part, slot, ring=0, by=1):
        return remote(
            self.region(half, first, second, part), self.slot_ref(half, slot, part),
            self.send_sem.at[half, sem], self.recv_sem.at[half, sem],
            self.place.neighbour(half, ring, by),
        )

    def plan(self):
        found = {}
        for i, second in enumerate((2, 3, 1, 0)):
            found[4 * i] = ((2, second), 1, i, 0, 1)
            found[4 * i + 1] = ((2, second), 2, i, 0, 3)
            found[4 * i + 2] = ((1, second), 0, 4 + i, 0, 1)
            found[4 * i + 3] = ((3, second), 0, 8 + i, 0, 3)
        found[16] = ((0, 2), 1, 12, 1, 1)
        found[17] = ((0, 2), 2, 12, 1, 3)
        found[18] = ((0, 1), 0, 13, 1, 1)
        found[19] = ((0, 3), 0, 14, 1, 3)
        return found

    def send(self, half, *sems):
        for sem in sems:
            block, part, slot, ring, by = self.plan()[sem]
            self.copy(half, sem, *block, part, slot, ring, by).start()

    def wait(self, half, *sems):
        for sem in sems:
            block, part, slot, ring, by = self.plan()[sem]
            self.copy(half, sem, *block, part, slot, ring, by).wait_recv()

    def wait_sent(self):
        for half in range(2):
            for sem, (block, part, slot, ring, by) in self.plan().items():
                self.copy(half, sem, *block, part, slot, ring, by).wait_send()

    def add(self, half, first, second, part, *slots):
        ref = self.region(half, first, second, part)
        value = ref[...].astype(F32)
        for slot in slots:
            value += self.slot_ref(half, slot, part)[...].astype(F32)
        ref[...] = value.astype(BF16)

    def finish(self, half):
        lo, hi = self.columns(half, 0)
        value = self.region(half, 0, 0, 0)[...].astype(F32)
        for slot in (13, 14):
            value += self.slot_ref(half, slot, 0)[...].astype(F32)
        self.total[:, lo:hi] = value.astype(BF16)

        @pl.when(self.place.moved)
        def _():
            self.moved(half).start()

    def moved(self, half):
        lo, hi = self.columns(half, 0)
        return remote(
            self.total.at[:, lo:hi], self.result.at[:, lo:hi],
            self.send_sem.at[half, 20], self.recv_sem.at[half, 20], self.place.partner,
        )

    def put(self, out_ref):
        @pl.when(self.place.moved)
        def _():
            for half in range(2):
                self.moved(half).wait()
            out_ref[...] = self.result[...]

        @pl.when(jnp.logical_not(self.place.moved))
        def _():
            out_ref[...] = self.total[...]


def reduce(parts):
    pairs = [(part, half) for part in parts for half in range(2)]
    for i in range(4):
        for part, half in pairs:
            part.send(half, 4 * i, 4 * i + 1)
    for i, second in enumerate((2, 3, 1, 0)):
        for part, half in pairs:
            part.wait(half, 4 * i)
            part.add(half, 1, second, 1, i)
            part.send(half, 4 * i + 2)
            part.wait(half, 4 * i + 1)
            part.add(half, 3, second, 2, i)
            part.send(half, 4 * i + 3)
    for i, second in enumerate((2, 3, 1, 0)):
        for part, half in pairs:
            part.wait(half, 4 * i + 2, 4 * i + 3)
            part.add(half, 0, second, 0, 4 + i, 8 + i)
            if i == 0:
                part.send(half, 16, 17)
            elif i == 1:
                part.wait(half, 17)
                part.add(half, 0, 3, 2, 12)
                part.send(half, 19)
            elif i == 2:
                part.wait(half, 16)
                part.add(half, 0, 1, 1, 12)
                part.send(half, 18)
    for part, half in pairs:
        part.wait(half, 18, 19)
        part.finish(half)


def head_probs(proj, bias, head):
    lo = head * HEAD
    queries = proj[:, lo : lo + HEAD]
    keys = proj[:, HD + lo : HD + lo + HEAD]
    scores = dot(queries, keys, ((1,), (1,))) * SCALE + bias
    shifted = jnp.exp(scores - jnp.max(scores, -1, keepdims=True))
    return shifted / jnp.sum(shifted, -1, keepdims=True)


def forward_kernel(
    start_ref, member_ref, permitted_ref, qkv_shard, out_shard, hint_shard,
    control_ref, after_ref, proj_ref, att_ref, bias_ref, term_ref, qkv_ref, out_ref, hint_ref,
    landed, leaving, acc, member, permitted, qkv, out, hint,
    hop_send, hop_recv, small_send, small_recv, start_sem, copy_sem,
    qkv_send, qkv_recv, qkv_own, out_send, out_recv, out_own, hint_send, hint_recv, hint_own,
    go_sem,
):
    place = Place()
    section, core = place.section, place.core
    kept = jnp.logical_not(place.moved)
    place.greet()

    def member_copy():
        return remote(member_ref, member, small_send.at[0], small_recv.at[0], place.sibling)

    def permitted_copy():
        return remote(permitted_ref, permitted, small_send.at[1], small_recv.at[1], place.partner)

    def start_copy(k):
        return pltpu.make_async_copy(
            start_ref.at[:, k * CW : (k + 1) * CW], landed.at[k], start_sem.at[k]
        )

    def start_across(k):
        return remote(
            start_ref.at[:, k * CW : (k + 1) * CW], landed.at[k],
            hop_send.at[k], hop_recv.at[k], place.sibling,
        )

    def hop(k):
        return remote(leaving.at[k], landed.at[k], hop_send.at[k], hop_recv.at[k], place.later)

    @pl.when(kept)
    def _():
        member_copy().start()
        member[...] = member_ref[...]
        permitted[...] = permitted_ref[...]

    @pl.when(place.moved)
    def _():
        permitted_copy().start()

    first_here = (section == 0) & kept
    first_given = (section == 4) & kept & (place.xlo == 1)

    @pl.when(first_here)
    def _():
        for k in range(CH):
            start_copy(k).start()

    @pl.when((place.z == 0) & (place.xlo == 1) & (core == 1))
    def _():
        for k in range(CH):
            start_across(k).start()

    qkv_gather = Gather(place, qkv_shard, qkv, QKV_CUT, qkv_send, qkv_recv, qkv_own)
    out_gather = Gather(place, out_shard, out, OUT_CUT, out_send, out_recv, out_own)
    hint_gather = Gather(place, hint_shard, hint, HINT_CUT, hint_send, hint_recv, hint_own)

    start_own([qkv_gather, out_gather])

    @pl.when(core == 1)
    def _():
        pl.semaphore_wait(go_sem, 1)

    gather([qkv_gather, out_gather])

    @pl.when(core == 0)
    def _():
        pl.semaphore_signal(go_sem, inc=1, device_id=place.sibling, device_id_type=MESH)

    start_own([hint_gather])
    keep_qkv = pltpu.make_async_copy(qkv, qkv_ref, copy_sem.at[0])
    keep_out = pltpu.make_async_copy(out, out_ref, copy_sem.at[1])
    keep_hint = pltpu.make_async_copy(hint, hint_ref, copy_sem.at[2])
    keep_qkv.start()
    keep_out.start()

    @pl.when(place.moved)
    def _():
        member_copy().wait_recv()
        permitted_copy().wait_recv()

    pairs = dot(dot(member[...], permitted[...]).astype(BF16), member[...], ((1,), (1,)))
    bias_ref[...] = jnp.where(pairs > 0.5, 0.0, -1e30)

    @pl.when(core == 1)
    def _():
        gather([hint_gather])

    squares = jnp.zeros((ROWS, 1), F32)
    for k in range(CH):
        @pl.when(first_here)
        def _():
            start_copy(k).wait()

        @pl.when(jnp.logical_not(first_here))
        def _():
            hop(k).wait_recv()

        x = landed[k]
        wide = x.astype(F32)
        squares += jnp.sum(wide * wide, -1, keepdims=True)
        for n in range(3):
            cols = slice(n * HD, (n + 1) * HD)
            part = dot(x, qkv[k * CW : (k + 1) * CW, cols])
            if k == 0:
                acc[:, cols] = part
            elif k < CH - 1:
                acc[:, cols] += part
            else:
                inverse = lax.rsqrt(squares * (1.0 / WIDTH) + 1e-06)
                proj_ref[:, cols] = ((acc[:, cols] + part) * inverse).astype(BF16)
    bias = bias_ref[...]
    for h in range(HEADS):
        probs = head_probs(proj_ref, bias, h).astype(BF16)
        lo = 2 * HD + h * HEAD
        att_ref[:, h * HEAD : (h + 1) * HEAD] = dot(probs, proj_ref[:, lo : lo + HEAD]).astype(BF16)
    att = att_ref[...]

    @pl.when(first_given)
    def _():
        for k in range(CH):
            start_across(k).wait_send()

    for k in range(CH):
        value = landed[k].astype(F32) + dot(att, out[:, k * CW : (k + 1) * CW])
        leaving[k] = value.astype(BF16)

        @pl.when(section < 7)
        def _():
            hop(k).start()

    control_ref[...] = landed[...]
    after_ref[...] = leaving[...]

    @pl.when(core == 0)
    def _():
        gather([hint_gather])

    keep_hint.start()
    for n in range(FEAT // 512):
        cols = slice(n * 512, (n + 1) * 512)
        value = dot(leaving[0], hint[0:CW, cols])
        for k in range(1, CH):
            value += dot(leaving[k], hint[k * CW : (k + 1) * CW, cols])
        term_ref[:, cols] = value

    @pl.when(kept)
    def _():
        member_copy().wait_send()

    @pl.when(place.moved)
    def _():
        permitted_copy().wait_send()

    @pl.when(section < 7)
    def _():
        for k in range(CH):
            hop(k).wait_send()

    qkv_gather.wait_sent()
    out_gather.wait_sent()
    hint_gather.wait_sent()
    keep_qkv.wait()
    keep_out.wait()
    keep_hint.wait()


def backward_kernel(
    hint_ref, control_ref, proj_ref, bias_ref, wqkv_ref, wout_ref, att_ref, next_ref, summed_ref,
    sum_qkv, sum_out, sum_hint,
    landed, leaving, probs_ref, acc, after, gproj,
    normed_t, att_t, next_t,
    grad_qkv, grad_out, grad_hint, land_qkv, land_out, land_hint,
    tot_qkv, tot_out, tot_hint, res_qkv, res_out, res_hint,
    hop_send, hop_recv,
    qkv_send, qkv_recv, out_send, out_recv, hint_send, hint_recv,
):
    place = Place()
    section, core = place.section, place.core
    place.greet()
    red_qkv = Reduce(place, grad_qkv, land_qkv, tot_qkv, res_qkv, QKV_CUT, qkv_send, qkv_recv)
    red_out = Reduce(place, grad_out, land_out, tot_out, res_out, OUT_CUT, out_send, out_recv)
    red_hint = Reduce(place, grad_hint, land_hint, tot_hint, res_hint, HINT_CUT, hint_send, hint_recv)

    bias = bias_ref[...]
    for h in range(HEADS):
        probs_ref[h] = head_probs(proj_ref, bias, h)
    squares = jnp.zeros((ROWS, 1), F32)
    for k in range(CH):
        wide = control_ref[k].astype(F32)
        squares += jnp.sum(wide * wide, -1, keepdims=True)
    inverse = lax.rsqrt(squares * (1.0 / WIDTH) + 1e-06)

    def hint_part():
        for k in range(CH):
            next_t[k * CW : (k + 1) * CW, :] = next_ref[k].T
        for m in range(CH):
            for n in range(FEAT // 512):
                cols = slice(n * 512, (n + 1) * 512)
                rows = slice(m * CW, (m + 1) * CW)
                grad_hint[rows, cols] = dot(next_t[rows, :], summed_ref[:, cols]).astype(BF16)
        reduce([red_hint])

    @pl.when(core == 0)
    def _():
        hint_part()

    for k in range(CH):
        normed = (control_ref[k].astype(F32) * inverse).astype(BF16)
        normed_t[k * CW : (k + 1) * CW, :] = normed.T
    for k in range(HD // CW):
        att_t[k * CW : (k + 1) * CW, :] = att_ref[:, k * CW : (k + 1) * CW].T

    def hop(k):
        return remote(leaving.at[k], landed.at[k], hop_send.at[k], hop_recv.at[k], place.earlier)

    @pl.when(section == 7)
    def _():
        for k in range(CH):
            landed[k] = jnp.zeros((ROWS, CW), BF16)

    for k in range(CH):
        @pl.when(section < 7)
        def _():
            hop(k).wait_recv()

        grad = (landed[k].astype(F32) + hint_ref[k]).astype(BF16)
        after[k] = grad
        part = dot(grad, wout_ref[:, k * CW : (k + 1) * CW], ((1,), (1,)))
        if k == 0:
            acc[...] = part
        else:
            acc[...] += part
    through = jnp.zeros((ROWS, 1), F32)
    for h in range(HEADS):
        lo = h * HEAD
        grad_att = acc[:, lo : lo + HEAD].astype(BF16)
        queries = proj_ref[:, lo : lo + HEAD]
        keys = proj_ref[:, HD + lo : HD + lo + HEAD]
        values = proj_ref[:, 2 * HD + lo : 2 * HD + lo + HEAD]
        probs = probs_ref[h]
        grad_probs = dot(grad_att, values, ((1,), (1,)))
        grad_values = dot(probs.astype(BF16), grad_att, ((0,), (0,))).astype(BF16)
        total = jnp.sum(grad_probs * probs, -1, keepdims=True)
        grad_scores = (probs * (grad_probs - total) * SCALE).astype(BF16)
        grad_queries = dot(grad_scores, keys).astype(BF16)
        grad_keys = dot(grad_scores, queries, ((0,), (0,))).astype(BF16)
        for n, (grad, value) in enumerate(
            ((grad_queries, queries), (grad_keys, keys), (grad_values, values))
        ):
            gproj[:, n * HD + lo : n * HD + lo + HEAD] = grad
            through += jnp.sum(grad.astype(F32) * value.astype(F32), -1, keepdims=True)
    slope = inverse * inverse * through * (1.0 / WIDTH)

    @pl.when(section > 0)
    def _():
        grad_proj = gproj[...]
        for k in range(CH):
            grad_normed = dot(grad_proj, wqkv_ref[k * CW : (k + 1) * CW, :], ((1,), (1,)))
            value = after[k].astype(F32) + inverse * grad_normed - control_ref[k].astype(F32) * slope
            leaving[k] = value.astype(BF16)
            hop(k).start()

    for m in range(CH):
        rows = slice(m * CW, (m + 1) * CW)
        for n in range(3):
            cols = slice(n * HD, (n + 1) * HD)
            grad_qkv[rows, cols] = dot(normed_t[rows, :], gproj[:, cols]).astype(BF16)
    for m in range(HD // CW):
        rows = slice(m * CW, (m + 1) * CW)
        for n in range(CH):
            grad_out[rows, n * CW : (n + 1) * CW] = dot(att_t[rows, :], after[n]).astype(BF16)
    reduce([red_qkv, red_out])

    @pl.when(core == 1)
    def _():
        hint_part()

    red_qkv.put(sum_qkv)
    red_out.put(sum_out)
    red_hint.put(sum_hint)

    @pl.when(section > 0)
    def _():
        for k in range(CH):
            hop(k).wait_send()

    red_qkv.wait_sent()
    red_out.wait_sent()
    red_hint.wait_sent()


def dma_sems(*shape):
    return pltpu.SemaphoreType.DMA(shape)


def kernel_call(kernel, ins, outs, scratch, collective_id, flops):
    spaces = {"v": pltpu.VMEM, "a": pl.ANY}
    return pl.pallas_call(
        kernel,
        out_shape=[shape for shape, _ in outs],
        in_specs=[pl.BlockSpec(memory_space=spaces[kind]) for kind in ins],
        out_specs=[pl.BlockSpec(memory_space=spaces[kind]) for _, kind in outs],
        scratch_shapes=scratch,
        compiler_params=pltpu.CompilerParams(
            collective_id=collective_id, has_side_effects=True, vmem_limit_bytes=VMEM_LIMIT
        ),
        cost_estimate=pl.CostEstimate(flops=flops, bytes_accessed=12_000_000, transcendentals=0),
    )


def chunked(value):
    return value.reshape(ROWS, CH, CW).transpose(1, 0, 2)


def flat(value):
    return value.transpose(1, 0, 2).reshape(ROWS, WIDTH)


def swap_roles(value):
    return lax.ppermute(value, ("xlo", "core"), [(0, 0), (1, 2), (2, 1), (3, 3)])


def of_clip(value):
    other = lax.ppermute(value, "core", [(0, 1), (1, 0)])
    return jnp.where(lax.axis_index("core") == lax.axis_index("xlo"), value, other)


def tile_members(layout):
    holds = layout[None, :] == jnp.arange(ROWS)[:, None]
    tile_of = jnp.sum(jnp.where(holds, jnp.arange(ROWS)[None, :] // TILE, 0), 1)
    return (tile_of[:, None] == jnp.arange(128)[None, :]).astype(BF16)


def permitted_tiles(offset, mask):
    row_tile = jnp.arange(4)[:, None]
    col_tile = jnp.arange(4)[None, :]
    near_window = jnp.abs(col_tile - row_tile - offset[:, None]) <= 1
    permitted = (row_tile == col_tile) | near_window & (mask == 1)
    return jnp.pad(permitted.astype(BF16), ((0, 124), (0, 124)))


def shape_of(*dims, dtype=BF16):
    return jax.ShapeDtypeStruct(dims, dtype)


def shards(
    control_in, base_in, base_update, out_gain, cotangent,
    w_qkv, w_out, w_hint, window_offset, tile_mask, token_layout,
):
    member = tile_members(token_layout[0])
    permitted = permitted_tiles(window_offset[0], tile_mask[0])
    chunks = (CH, ROWS, CW)

    control_s, control_next, proj, att, bias, term, weight_qkv, weight_out, weight_hint = kernel_call(
        forward_kernel,
        "avvaaa",
        [
            (shape_of(*chunks), "v"),
            (shape_of(*chunks), "v"),
            (shape_of(ROWS, QKV), "v"),
            (shape_of(ROWS, HD), "v"),
            (shape_of(ROWS, ROWS, dtype=F32), "v"),
            (shape_of(ROWS, FEAT, dtype=F32), "v"),
            (shape_of(WIDTH, QKV), "a"),
            (shape_of(HD, WIDTH), "a"),
            (shape_of(WIDTH, FEAT), "a"),
        ],
        [
            pltpu.VMEM(chunks, BF16),
            pltpu.VMEM(chunks, BF16),
            pltpu.VMEM((ROWS, QKV), F32),
            pltpu.VMEM((ROWS, 128), BF16),
            pltpu.VMEM((128, 128), BF16),
            pltpu.VMEM((WIDTH, QKV), BF16),
            pltpu.VMEM((HD, WIDTH), BF16),
            pltpu.VMEM((WIDTH, FEAT), BF16),
            dma_sems(CH), dma_sems(CH), dma_sems(2), dma_sems(2), dma_sems(CH), dma_sems(3),
            dma_sems(2, 21), dma_sems(2, 21), dma_sems(2),
            dma_sems(2, 21), dma_sems(2, 21), dma_sems(2),
            dma_sems(2, 21), dma_sems(2, 21), dma_sems(2),
            pltpu.SemaphoreType.REGULAR,
        ],
        1,
        100_000_000_000,
    )(control_in, member, permitted, w_qkv[0], w_out[0], w_hint[0])

    base = of_clip(base_in)
    cot = of_clip(cotangent)
    update = swap_roles(base_update[0])
    term = term + update.astype(F32)
    summed = base.astype(F32) + lax.psum(term.astype(BF16), ("z", "core")).astype(F32)

    inverse = lax.rsqrt(jnp.mean(summed * summed, -1, keepdims=True) + 1e-06)
    grad_normed = cot.astype(F32) * out_gain
    grad_summed = (
        inverse * grad_normed
        - summed * inverse**3 * jnp.mean(grad_normed * summed, -1, keepdims=True)
    ).astype(BF16)

    mine = swap_roles(summed.astype(BF16)).astype(F32)
    features = mine * lax.rsqrt(jnp.mean(mine * mine, -1, keepdims=True) + 1e-06) * out_gain

    hint_grad = dot(grad_summed, weight_hint, ((1,), (1,)))

    sum_qkv, sum_out, sum_hint = kernel_call(
        backward_kernel,
        "vvvvvvvvv",
        [
            (shape_of(96, QKV), "v"),
            (shape_of(48, WIDTH), "v"),
            (shape_of(96, FEAT), "v"),
        ],
        [
            pltpu.VMEM(chunks, BF16),
            pltpu.VMEM(chunks, BF16),
            pltpu.VMEM((HEADS, ROWS, ROWS), F32),
            pltpu.VMEM((ROWS, HD), F32),
            pltpu.VMEM(chunks, BF16),
            pltpu.VMEM((ROWS, QKV), BF16),
            pltpu.VMEM((WIDTH, ROWS), BF16),
            pltpu.VMEM((HD, ROWS), BF16),
            pltpu.VMEM((WIDTH, ROWS), BF16),
            pltpu.VMEM((WIDTH, QKV), BF16),
            pltpu.VMEM((HD, WIDTH), BF16),
            pltpu.VMEM((WIDTH, FEAT), BF16),
            pltpu.VMEM((2, 15, 96, QKV // 2), BF16),
            pltpu.VMEM((2, 15, 48, WIDTH // 2), BF16),
            pltpu.VMEM((2, 15, 96, FEAT // 2), BF16),
            pltpu.VMEM((96, QKV), BF16),
            pltpu.VMEM((48, WIDTH), BF16),
            pltpu.VMEM((96, FEAT), BF16),
            pltpu.VMEM((96, QKV), BF16),
            pltpu.VMEM((48, WIDTH), BF16),
            pltpu.VMEM((96, FEAT), BF16),
            dma_sems(CH), dma_sems(CH),
            dma_sems(2, 21), dma_sems(2, 21),
            dma_sems(2, 21), dma_sems(2, 21),
            dma_sems(2, 21), dma_sems(2, 21),
        ],
        2,
        100_000_000_000,
    )(
        chunked(hint_grad), control_s, proj, bias, weight_qkv, weight_out, att, control_next,
        grad_summed,
    )
    factor = 4096.0 ** (-0.5)
    return (
        features,
        (sum_qkv.astype(F32) * factor)[None],
        (sum_out.astype(F32) * factor)[None],
        (sum_hint.astype(F32) * factor)[None],
    )


def solution(mesh):
    parts = jax.sharding.Mesh(
        mesh.devices.reshape(2, 4, 2, 4, 2), ("xlo", "z", "xhi", "y", "core")
    )
    segment = ("xlo", "z")
    dp = ("xhi", "y", "core")
    by_rows = P(dp, None)
    by_both = P(segment, dp, None)
    placed = (
        by_rows, by_rows, by_both, P(), by_rows, by_both, by_both, by_both,
        P(segment, None), P(segment, None, None), by_rows,
    )
    return jax.shard_map(
        shards,
        mesh=parts,
        in_specs=placed,
        out_specs=(by_rows, by_both, by_both, by_both),
        check_vma=False,
    )
```

time: 1050 us -> 463 us (0.44)
  waiting for transfers between devices: 745 us -> 105 us
  Pallas kernels: 138 us -> 312 us
  starting transfers between devices: 96.2 us -> 7.04 us
  matrix products: 22.7 us -> 2.24 us
  local copies, waits for them, and re-layouts: 16.3 us -> 2.69 us
    reduce_scatter x3 -> x0, waiting for transfers between devices: 330 us -> none  [the longest x1 169 us: shards(): lax.psum_scatter(grad_hint, plane, scatter_dimension=0, tiled=True)]
    all_gather x3 -> x0, waiting for transfers between devices: 281 us -> none  [the longest x1 158 us: shards(): weight_qkv = lax.all_gather(swap_roles(w_qkv[0]), plane, axis=0, tiled=True)]
    pallas_call x2, Pallas kernels: 138 us -> 312 us  [the longest x1 162 us: shards(): kernel_call(backward_kernel, 'vvvvvvvvv', [(shape_of(96, QKV), 'v'), (sha...]
    ppermute x9 -> x2, starting transfers between devices: 87.1 us -> 6.42 us  [swap_roles(): lax.ppermute(value, ('xlo', 'core'), [(0, 0), (1, 2), (2, 1), (3, 3)])]
    ppermute x9 -> x2, waiting for transfers between devices: 71.8 us -> 13 us  [swap_roles(): lax.ppermute(value, ('xlo', 'core'), [(0, 0), (1, 2), (2, 1), (3, 3)])]
    psum x1, waiting for transfers between devices: 62.5 us -> 92.1 us  [shards(): lax.psum(term.astype(BF16), ('z', 'core')).astype(F32)]
    dot_general x6 -> x1, matrix products: 22.7 us -> 2.24 us  [dot(): return lax.dot_general(a, b, (dims, ((), ())), preferred_element_type=F32)]
  transfers between devices with their start and end apart: 20 -> 5, of which waited for: 12 -> 2; matrix products, arithmetic and copies ran while one was open for 3% -> 2% of each run, Pallas kernels for 7% -> 33%
where the time goes in v2:
time: 463 us
  Pallas kernels  312 us (67%)
  waiting for transfers between devices  105 us (23%)
  other arithmetic  19.6 us (4%)
  between operations  14.2 us (3%)
  starting transfers between devices  7.04 us (2%)
    pallas_call x1, Pallas kernels, shards(): kernel_call(backward_kernel, 'vvvvvvvvv', [(shape_of(96, QKV), 'v'), (sha...  162 us
    pallas_call x1, Pallas kernels, shards(): kernel_call(forward_kernel, 'avvaaa', [(shape_of(*chunks), 'v'), (shape_o...  150 us
    psum x1, waiting for transfers between devices, shards(): lax.psum(term.astype(BF16), ('z', 'core')).astype(F32)  92.1 us
    ppermute x2, waiting for transfers between devices, swap_roles(): lax.ppermute(value, ('xlo', 'core'), [(0, 0), (1, 2), (2, 1), (3, 3)])  13 us
  transfers between devices with their start and end apart: 5, of which 2 were waited for; matrix products, arithmetic and copies ran while one was open for 2% of the time, Pallas kernels for 33%

profile of v2, /device:TPU:1, one launch (start us, length us, event | category | flops | bytes accessed | tf_op | source)
XLA Modules:
  0.0 462.9 jit_solution(5832494891440390239)
XLA Ops:
  7.2 0.0 all-reduce.3.cloned.1.call-start
  7.2 4.5 collective-permute-start.1
  11.7 0.1 collective-permute-start.3
  11.8 0.5 collective-permute-start
  12.3 0.8 select_reduce_fusion
  13.1 0.7 fusion.3.member_ref
  13.9 0.8 fusion.5
  14.6 0.6 pad_convert_fusion.permitted_ref
  15.2 150.5 %shard_map.138 = (bf16[6,256,256]{2,1,0:T(8,128)(2,1)}, bf16[6,256,256]{2,1,0:T(8,128)(2,1)}, bf16[256,2304]{1,0:T(8,128)(2,1)}, bf16[256,768]{1,0:T(8,128)(2,1)...) custom-call(bf16[256,1536]{1,0:T(8,128)(2,1)} %start_ref.1, ...), custom_call_target="tpu_custom_call" | custom-call | flops 99999997952 | bytes 12000000 | tf_op jit(solution)/shard_map/pallas_call | solution.py:705
  165.7 0.0 collective-permute-done.1
  165.7 0.0 copy-start.2
  165.8 1.0 copy-done.2
  166.8 3.6 add_convert_fusion
  170.4 0.0 all-reduce.3.cloned.1.call-update
  170.4 0.0 collective-permute-done.3
  170.4 0.0 collective-permute-done
  170.4 92.1 %all-reduce.3.cloned.1.call-done = bf16[256,2560]{1,0:T(8,128)(2,1)} async-done(((bf16[256,2560]{1,0:T(8,128)(2,1)}), bf16[256,2560]{1,0:T(8,128)(2,1)}) %all-reduce.3.cloned.1.call-update) | async-done | bytes 1310736 | tf_op jit(solution)/shard_map/psum | solution.py:742
  262.5 0.0 copy-done
  262.5 0.0 copy-done.5
  262.5 3.2 multiply_reduce_fusion.1
  265.7 0.0 slice-start.1
  265.7 2.1 subtract_convert_fusion
  267.9 2.2 fusion.6
  270.1 1.6 copy.18
  271.7 161.6 %shard_map.139 = (bf16[96,2304]{1,0:T(8,128)(2,1)}, bf16[48,1536]{1,0:T(8,128)(2,1)}, bf16[96,2560]{1,0:T(8,128)(2,1)}) custom-call(f32[6,256,256]{2,1,0:T(8,128)} %bitcast.18, bf16[6,256,256]{2,1,0:T(8,128)(2,1)} %get-tuple-element.18.control_ref, bf16[256,2304]{1,0:T(8,128)(2,1)} %get-tuple-element.19.proj_ref, f32[256,256]{1,0:T(8,128)} %get-tuple-element.20.bias_ref, ...), custom_call_target="tpu_custom_call" | custom-call | flops 99999997952 | bytes 12000000 | tf_op jit(solution)/shard_map/pallas_call | solution.py:756
  433.3 1.6 multiply_bitcast_fusion.2
  434.9 1.9 collective-permute-start.2
  436.9 2.1 multiply_bitcast_fusion
  438.9 2.0 multiply_bitcast_fusion.1
  440.9 13.0 %collective-permute-done.2 = bf16[256,2560]{1,0:T(8,128)(2,1)S(1)} collective-permute-done((bf16[256,2560]{1,0:T(8,128)(2,1)S(1)}, bf16[256,2560]{1,0:T(8,128)(2,1)S(1)}, u32[]{:S(2)}, u32[]{:S(2)}) %collective-permute-start.2) | collective-permute-done | bytes 1310752 | tf_op jit(solution)/shard_map/ppermute | solution.py:671
  453.9 0.3 fusion
  454.2 1.8 fusion.1
  (15 shorter events, 0.0 us)
Async XLA Ops:
  7.2 255.4 %all-reduce.3.cloned.1.call-start = ((), (), s32[]{:S(2)}) async-start(), calls=%async_computation | async-start | bytes 2621440 | tf_op jit(solution)/shard_map/psum | solution.py:742
  7.2 158.5 %collective-permute-start.1 = (bf16[256,2560]{1,0:T(8,128)(2,1)}, bf16[256,2560]{1,0:T(8,128)(2,1)S(1)}, u32[]{:S(2)}, u32[]{:S(2)}) collective-permute-start(bf16[256,2560]{1,0:T(8,128)(2,1)} %bitcast.22), channel_id=1, source_target_pairs={{0,0},{1,64},{64,1},{65,65},{2,2},{3,66},{66,3},{67,67},{4,4},{5,6... | collective-permute-start | bytes 3932168 | tf_op jit(solution)/shard_map/ppermute | solution.py:671
  11.7 158.7 %collective-permute-start.3 = (bf16[256,2560]{1,0:T(8,128)(2,1)}, bf16[256,2560]{1,0:T(8,128)(2,1)S(1)}, u32[]{:S(2)}, u32[]{:S(2)}) collective-permute-start(bf16[256,2560]{1,0:T(8,128)(2,1)} %param.15), channel_id=1, source_target_pairs={{0,1},{1,0},{2,3},{3,2},{4,5},{5,4},{6,7},{7,6},{8,9},{9,8},{10,11... | collective-permute-start | bytes 3932168 | tf_op jit(solution)/shard_map/ppermute | solution.py:675
  11.8 158.6 %collective-permute-start = (bf16[256,2560]{1,0:T(8,128)(2,1)}, bf16[256,2560]{1,0:T(8,128)(2,1)}, u32[]{:S(2)}, u32[]{:S(2)}) collective-permute-start(bf16[256,2560]{1,0:T(8,128)(2,1)} %param.12), channel_id=1, source_target_pairs={{0,1},{1,0},{2,3},{3,2},{4,5},{5,4},{6,7},{7,6},{8,9},{9,8},{10,11... | collective-permute-start | bytes 3932168 | tf_op jit(solution)/shard_map/ppermute | solution.py:675
  165.7 1.1 copy-start.2
  166.8 95.7 %copy-start = (bf16[256,2560]{1,0:T(8,128)(2,1)S(1)}, bf16[256,2560]{1,0:T(8,128)(2,1)}, u32[]{:S(2)}) copy-start(bf16[256,2560]{1,0:T(8,128)(2,1)} %param.15) | copy-start | bytes 3932164
  166.8 95.7 %copy-start.5 = (f32[2560]{0:T(1024)S(1)}, f32[2560]{0:T(1024)}, u32[]{:S(2)}) copy-start(f32[2560]{0:T(1024)} %param.14) | copy-start | bytes 30724
  262.5 3.2 copy-start.1
  262.5 5.3 %slice-start = ((s8[7864320]{0:T(1024)(128)(4,1)}), s8[4194304]{0:T(1024)(128)(4,1)S(1)}, s32[]{:S(2)}) async-start(s8[7864320]{0:T(1024)(128)(4,1)} %bitcast.26), calls=%async_computation.1 | async-start | bytes 8388608
  265.7 2.1 slice-start.1
  267.8 2.3 copy-start.4
  271.7 163.2 %copy-start.3 = (bf16[256,2560]{1,0:T(8,128)(2,1)S(1)}, bf16[256,2560]{1,0:T(8,128)(2,1)}, u32[]{:S(2)}) copy-start(bf16[256,2560]{1,0:T(8,128)(2,1)} %get-tuple-element.32) | copy-start | bytes 3932164
  434.9 18.9 %collective-permute-start.2 = (bf16[256,2560]{1,0:T(8,128)(2,1)S(1)}, bf16[256,2560]{1,0:T(8,128)(2,1)S(1)}, u32[]{:S(2)}, u32[]{:S(2)}) collective-permute-start(bf16[256,2560]{1,0:T(8,128)(2,1)S(1)} %copy-done.3), channel_id=1, source_target_pairs={{0,0},{1,64},{64,1},{65,65},{2,2},{3,66},{66,3},{67,67},{4,4},{5,6... | collective-permute-start | bytes 3932168 | tf_op jit(solution)/shard_map/ppermute | solution.py:671
Sparse Core Ops, SparseCore 0:
  170.5 91.9 all-reduce.2

commit v3 on v2

--- a/solution.py
+++ b/solution.py
@@ -63,10 +63,10 @@
         return (x // 2) * 8 + y * 2 + lax.rem(x, 2)
 
     def greet(self):
-        others = (
-            self.later, self.earlier, self.sibling, self.partner,
-            self.along_x(1), self.along_x(3), self.along_y(1), self.along_y(3),
-        )
+        others = [self.partner, self.along_x(1), self.along_x(3), self.along_y(1), self.along_y(3)]
+        for by in range(1, 8):
+            other = lax.rem(self.section + by, 8)
+            others.append({"z": lax.rem(other, 4), "core": other // 4})
         barrier = pltpu.get_barrier_semaphore()
         for other in others:
             pl.semaphore_signal(barrier, inc=1, device_id=other, device_id_type=MESH)
@@ -213,9 +213,8 @@
 
 
 class Reduce:
-    def __init__(self, place, grad, landing, total, result, cut, send_sem, recv_sem):
-        self.place, self.grad, self.landing = place, grad, landing
-        self.total, self.result = total, result
+    def __init__(self, place, grad, landing, result, cut, send_sem, recv_sem):
+        self.place, self.grad, self.landing, self.result = place, grad, landing, result
         self.rows, self.cuts = cut
         self.send_sem, self.recv_sem = send_sem, recv_sem
 
@@ -275,11 +274,7 @@
         ref[...] = value.astype(BF16)
 
     def finish(self, half):
-        lo, hi = self.columns(half, 0)
-        value = self.region(half, 0, 0, 0)[...].astype(F32)
-        for slot in (13, 14):
-            value += self.slot_ref(half, slot, 0)[...].astype(F32)
-        self.total[:, lo:hi] = value.astype(BF16)
+        self.add(half, 0, 0, 0, 13, 14)
 
         @pl.when(self.place.moved)
         def _():
@@ -288,20 +283,37 @@
     def moved(self, half):
         lo, hi = self.columns(half, 0)
         return remote(
-            self.total.at[:, lo:hi], self.result.at[:, lo:hi],
+            self.region(half, 0, 0, 0), self.result.at[:, lo:hi],
             self.send_sem.at[half, 20], self.recv_sem.at[half, 20], self.place.partner,
         )
 
-    def put(self, out_ref):
+    def put(self, out_ref, sem):
+        here = pltpu.make_async_copy(self.region_rows(), out_ref, sem)
+        across = pltpu.make_async_copy(self.result, out_ref, sem)
+
         @pl.when(self.place.moved)
         def _():
             for half in range(2):
                 self.moved(half).wait()
-            out_ref[...] = self.result[...]
+            across.start()
 
         @pl.when(jnp.logical_not(self.place.moved))
         def _():
-            out_ref[...] = self.total[...]
+            here.start()
+
+        def wait():
+            @pl.when(self.place.moved)
+            def _():
+                across.wait()
+
+            @pl.when(jnp.logical_not(self.place.moved))
+            def _():
+                here.wait()
+
+        return wait
+
+    def region_rows(self):
+        return self.grad.at[rows_of(self.place.block(0, 0, 0), self.rows), :]
 
 
 def reduce(parts):
@@ -345,12 +357,18 @@
     return shifted / jnp.sum(shifted, -1, keepdims=True)
 
 
-def forward_kernel(
+def section_kernel(
     start_ref, member_ref, permitted_ref, qkv_shard, out_shard, hint_shard,
-    control_ref, after_ref, proj_ref, att_ref, bias_ref, term_ref, qkv_ref, out_ref, hint_ref,
-    landed, leaving, acc, member, permitted, qkv, out, hint,
-    hop_send, hop_recv, small_send, small_recv, start_sem, copy_sem,
+    base_ref, cot_ref, update_ref, gain_ref,
+    mine_out, sum_qkv, sum_out, sum_hint,
+    landed, leaving, back_landed, back_leaving, after, acc, proj, att, gproj, probs, bias_ref,
+    member, permitted, qkv, out, hint, normed_t, att_t,
+    update, slots, gs, mine, mine_rows, base_rows, cot_rows,
+    land_qkv, land_out, land_hint, res_qkv, res_out, res_hint,
+    hop_send, hop_recv, back_send, back_recv, small_send, small_recv, start_sem, local_sem, out_sem,
     qkv_send, qkv_recv, qkv_own, out_send, out_recv, out_own, hint_send, hint_recv, hint_own,
+    rqkv_send, rqkv_recv, rout_send, rout_recv, rhint_send, rhint_recv,
+    term_send, term_recv, gs_send, gs_recv, mine_send, mine_recv,
     go_sem,
 ):
     place = Place()
@@ -364,6 +382,21 @@
     def permitted_copy():
         return remote(permitted_ref, permitted, small_send.at[1], small_recv.at[1], place.partner)
 
+    def row_copies(to_sibling):
+        owner = place.z + 4 * (1 - core) if to_sibling else section
+        for i, (src, dst) in enumerate(((base_ref, base_rows), (cot_ref, cot_rows))):
+            src = src.at[rows_of(owner, 32), :]
+            if to_sibling:
+                yield remote(src, dst, small_send.at[2 + i], small_recv.at[2 + i], place.sibling)
+            else:
+                yield pltpu.make_async_copy(src, dst, local_sem.at[i])
+
+    def update_across():
+        return remote(update_ref, update, small_send.at[4], small_recv.at[4], place.partner)
+
+    def update_here():
+        return pltpu.make_async_copy(update_ref, update, local_sem.at[2])
+
     def start_copy(k):
         return pltpu.make_async_copy(
             start_ref.at[:, k * CW : (k + 1) * CW], landed.at[k], start_sem.at[k]
@@ -378,35 +411,39 @@
     def hop(k):
         return remote(leaving.at[k], landed.at[k], hop_send.at[k], hop_recv.at[k], place.later)
 
-    @pl.when(kept)
-    def _():
-        member_copy().start()
-        member[...] = member_ref[...]
-        permitted[...] = permitted_ref[...]
-
-    @pl.when(place.moved)
-    def _():
-        permitted_copy().start()
-
     first_here = (section == 0) & kept
-    first_given = (section == 4) & kept & (place.xlo == 1)
-
-    @pl.when(first_here)
-    def _():
-        for k in range(CH):
-            start_copy(k).start()
-
-    @pl.when((place.z == 0) & (place.xlo == 1) & (core == 1))
-    def _():
-        for k in range(CH):
-            start_across(k).start()
+    first_given = (section == 4) & kept
 
     qkv_gather = Gather(place, qkv_shard, qkv, QKV_CUT, qkv_send, qkv_recv, qkv_own)
     out_gather = Gather(place, out_shard, out, OUT_CUT, out_send, out_recv, out_own)
     hint_gather = Gather(place, hint_shard, hint, HINT_CUT, hint_send, hint_recv, hint_own)
-
     start_own([qkv_gather, out_gather])
 
+    @pl.when(kept)
+    def _():
+        member_copy().start()
+        for copy in row_copies(True):
+            copy.start()
+        for copy in row_copies(False):
+            copy.start()
+        update_here().start()
+        member[...] = member_ref[...]
+        permitted[...] = permitted_ref[...]
+
+    @pl.when(place.moved)
+    def _():
+        permitted_copy().start()
+
+    @pl.when(first_here)
+    def _():
+        for k in range(CH):
+            start_copy(k).start()
+
+    @pl.when(first_given)
+    def _():
+        for k in range(CH):
+            start_across(k).start()
+
     @pl.when(core == 1)
     def _():
         pl.semaphore_wait(go_sem, 1)
@@ -418,11 +455,6 @@
         pl.semaphore_signal(go_sem, inc=1, device_id=place.sibling, device_id_type=MESH)
 
     start_own([hint_gather])
-    keep_qkv = pltpu.make_async_copy(qkv, qkv_ref, copy_sem.at[0])
-    keep_out = pltpu.make_async_copy(out, out_ref, copy_sem.at[1])
-    keep_hint = pltpu.make_async_copy(hint, hint_ref, copy_sem.at[2])
-    keep_qkv.start()
-    keep_out.start()
 
     @pl.when(place.moved)
     def _():
@@ -432,7 +464,11 @@
     pairs = dot(dot(member[...], permitted[...]).astype(BF16), member[...], ((1,), (1,)))
     bias_ref[...] = jnp.where(pairs > 0.5, 0.0, -1e30)
 
-    @pl.when(core == 1)
+    @pl.when(place.moved & (core == 1))
+    def _():
+        update_across().start()
+
+    @pl.when(section >= 6)
     def _():
         gather([hint_gather])
 
@@ -458,141 +494,213 @@
                 acc[:, cols] += part
             else:
                 inverse = lax.rsqrt(squares * (1.0 / WIDTH) + 1e-06)
-                proj_ref[:, cols] = ((acc[:, cols] + part) * inverse).astype(BF16)
+                proj[:, cols] = ((acc[:, cols] + part) * inverse).astype(BF16)
     bias = bias_ref[...]
     for h in range(HEADS):
-        probs = head_probs(proj_ref, bias, h).astype(BF16)
+        soft = head_probs(proj, bias, h)
+        probs[h] = soft
         lo = 2 * HD + h * HEAD
-        att_ref[:, h * HEAD : (h + 1) * HEAD] = dot(probs, proj_ref[:, lo : lo + HEAD]).astype(BF16)
-    att = att_ref[...]
+        value = dot(soft.astype(BF16), proj[:, lo : lo + HEAD])
+        att[:, h * HEAD : (h + 1) * HEAD] = value.astype(BF16)
 
     @pl.when(first_given)
     def _():
         for k in range(CH):
             start_across(k).wait_send()
 
+    attended = att[...]
     for k in range(CH):
-        value = landed[k].astype(F32) + dot(att, out[:, k * CW : (k + 1) * CW])
+        value = landed[k].astype(F32) + dot(attended, out[:, k * CW : (k + 1) * CW])
         leaving[k] = value.astype(BF16)
 
         @pl.when(section < 7)
         def _():
             hop(k).start()
 
-    control_ref[...] = landed[...]
-    after_ref[...] = leaving[...]
-
-    @pl.when(core == 0)
+    @pl.when(place.moved & (core == 0))
+    def _():
+        update_across().start()
+
+    @pl.when(section < 6)
     def _():
         gather([hint_gather])
 
-    keep_hint.start()
-    for n in range(FEAT // 512):
-        cols = slice(n * 512, (n + 1) * 512)
-        value = dot(leaving[0], hint[0:CW, cols])
-        for k in range(1, CH):
-            value += dot(leaving[k], hint[k * CW : (k + 1) * CW, cols])
-        term_ref[:, cols] = value
+    @pl.when(place.moved)
+    def _():
+        update_across().wait_recv()
 
     @pl.when(kept)
     def _():
-        member_copy().wait_send()
+        update_here().wait()
+
+    def along_column(by):
+        other = lax.rem(section + by, 8)
+        return other, {"z": lax.rem(other, 4), "core": other // 4}
+
+    def term_copy(by, half):
+        other, to = along_column(by)
+        cols = slice(half * 1280, (half + 1) * 1280)
+        return remote(
+            update.at[rows_of(other, 32), cols], slots.at[by, :, cols],
+            term_send.at[by, half], term_recv.at[by, half], to,
+        )
+
+    def gs_copy(by, owner):
+        rows = gs.at[rows_of(owner, 32), :]
+        return remote(rows, rows, gs_send.at[by], gs_recv.at[by], along_column(by)[1])
+
+    far_first = (4, 3, 5, 2, 6, 1, 7)
+    for half in range(2):
+        for n in range(2):
+            cols = slice(half * 1280 + n * 640, half * 1280 + (n + 1) * 640)
+            value = update[:, cols].astype(F32)
+            for k in range(CH):
+                value += dot(leaving[k], hint[k * CW : (k + 1) * CW, cols])
+            update[:, cols] = value.astype(BF16)
+        for by in far_first:
+            term_copy(by, half).start()
+
+    @pl.when(kept)
+    def _():
+        for copy in row_copies(False):
+            copy.wait()
 
     @pl.when(place.moved)
     def _():
-        permitted_copy().wait_send()
-
-    @pl.when(section < 7)
-    def _():
-        for k in range(CH):
-            hop(k).wait_send()
-
-    qkv_gather.wait_sent()
-    out_gather.wait_sent()
+        for copy in row_copies(True):
+            copy.wait_recv()
+
+    own_rows = rows_of(section, 32)
+    summed = base_rows[...].astype(F32) + update[own_rows, :].astype(F32)
+    for by in (1, 7, 2, 6, 3, 5, 4):
+        for half in range(2):
+            term_copy(by, half).wait_recv()
+        summed += slots[by].astype(F32)
+    inverse = lax.rsqrt(jnp.mean(summed * summed, -1, keepdims=True) + 1e-06)
+    grad_normed = cot_rows[...].astype(F32) * gain_ref[...]
+    slope = inverse * inverse * inverse * jnp.mean(grad_normed * summed, -1, keepdims=True)
+    gs[own_rows, :] = (inverse * grad_normed - summed * slope).astype(BF16)
+    for by in far_first:
+        gs_copy(by, section).start()
+    mine_rows[...] = summed.astype(BF16)
+
+    def mine_copy(by, kind, owner):
+        rows = mine.at[rows_of(owner, 32), :]
+        to = {"z": lax.rem(place.z + by, 4), "core": place.xlo}
+        return remote(mine_rows, rows, mine_send.at[by], mine_recv.at[by, kind], to)
+
+    def mine_across():
+        to = {"xlo": 1 - place.xlo}
+        return remote(mine, mine, mine_send.at[4], mine_recv.at[4, 0], to)
+
+    @pl.when(kept)
+    def _():
+        mine[own_rows, :] = summed.astype(BF16)
+        for by in (2, 1, 3):
+            mine_copy(by, 0, section).start()
+
+    @pl.when(place.moved)
+    def _():
+        for by in (2, 1, 3, 0):
+            mine_copy(by, 1, section).start()
+
     hint_gather.wait_sent()
-    keep_qkv.wait()
-    keep_out.wait()
-    keep_hint.wait()
-
-
-def backward_kernel(
-    hint_ref, control_ref, proj_ref, bias_ref, wqkv_ref, wout_ref, att_ref, next_ref, summed_ref,
-    sum_qkv, sum_out, sum_hint,
-    landed, leaving, probs_ref, acc, after, gproj,
-    normed_t, att_t, next_t,
-    grad_qkv, grad_out, grad_hint, land_qkv, land_out, land_hint,
-    tot_qkv, tot_out, tot_hint, res_qkv, res_out, res_hint,
-    hop_send, hop_recv,
-    qkv_send, qkv_recv, out_send, out_recv, hint_send, hint_recv,
-):
-    place = Place()
-    section, core = place.section, place.core
-    place.greet()
-    red_qkv = Reduce(place, grad_qkv, land_qkv, tot_qkv, res_qkv, QKV_CUT, qkv_send, qkv_recv)
-    red_out = Reduce(place, grad_out, land_out, tot_out, res_out, OUT_CUT, out_send, out_recv)
-    red_hint = Reduce(place, grad_hint, land_hint, tot_hint, res_hint, HINT_CUT, hint_send, hint_recv)
-
-    bias = bias_ref[...]
-    for h in range(HEADS):
-        probs_ref[h] = head_probs(proj_ref, bias, h)
-    squares = jnp.zeros((ROWS, 1), F32)
+    for by in (1, 7, 2, 6, 3, 5, 4):
+        gs_copy(by, lax.rem(section + 8 - by, 8)).wait_recv()
+
+    grad_sum = gs[...]
     for k in range(CH):
-        wide = control_ref[k].astype(F32)
-        squares += jnp.sum(wide * wide, -1, keepdims=True)
-    inverse = lax.rsqrt(squares * (1.0 / WIDTH) + 1e-06)
+        acc[:, k * CW : (k + 1) * CW] = dot(grad_sum, hint[k * CW : (k + 1) * CW, :], ((1,), (1,)))
+
+    red_qkv = Reduce(place, qkv, land_qkv, res_qkv, QKV_CUT, rqkv_send, rqkv_recv)
+    red_out = Reduce(place, out, land_out, res_out, OUT_CUT, rout_send, rout_recv)
+    red_hint = Reduce(place, hint, land_hint, res_hint, HINT_CUT, rhint_send, rhint_recv)
+
+    mine_keep = pltpu.make_async_copy(mine, mine_out, out_sem.at[3])
 
     def hint_part():
-        for k in range(CH):
-            next_t[k * CW : (k + 1) * CW, :] = next_ref[k].T
+        @pl.when(kept)
+        def _():
+            for by in range(4):
+                for kind in range(2):
+                    if (by, kind) != (0, 0):
+                        owner = lax.rem(place.z + 4 - by, 4) + 4 * (core if kind == 0 else 1 - core)
+                        mine_copy(by, kind, owner).wait_recv()
+            mine_across().start()
+
         for m in range(CH):
             for n in range(FEAT // 512):
                 cols = slice(n * 512, (n + 1) * 512)
                 rows = slice(m * CW, (m + 1) * CW)
-                grad_hint[rows, cols] = dot(next_t[rows, :], summed_ref[:, cols]).astype(BF16)
+                hint[rows, cols] = dot(leaving[m], gs[:, cols], ((0,), (0,))).astype(BF16)
         reduce([red_hint])
 
+        @pl.when(place.moved)
+        def _():
+            for by in (2, 1, 3, 0):
+                mine_copy(by, 1, section).wait_send()
+            mine_across().wait_recv()
+
+        mine_keep.start()
+
+    def transposes():
+        squares = jnp.zeros((ROWS, 1), F32)
+        for k in range(CH):
+            wide = landed[k].astype(F32)
+            squares += jnp.sum(wide * wide, -1, keepdims=True)
+        inverse = lax.rsqrt(squares * (1.0 / WIDTH) + 1e-06)
+        for k in range(CH):
+            normed = (landed[k].astype(F32) * inverse).astype(BF16)
+            normed_t[k * CW : (k + 1) * CW, :] = normed.T
+        for k in range(HD // CW):
+            att_t[k * CW : (k + 1) * CW, :] = att[:, k * CW : (k + 1) * CW].T
+
     @pl.when(core == 0)
     def _():
         hint_part()
-
+        transposes()
+
+    squares = jnp.zeros((ROWS, 1), F32)
     for k in range(CH):
-        normed = (control_ref[k].astype(F32) * inverse).astype(BF16)
-        normed_t[k * CW : (k + 1) * CW, :] = normed.T
-    for k in range(HD // CW):
-        att_t[k * CW : (k + 1) * CW, :] = att_ref[:, k * CW : (k + 1) * CW].T
-
-    def hop(k):
-        return remote(leaving.at[k], landed.at[k], hop_send.at[k], hop_recv.at[k], place.earlier)
+        wide = landed[k].astype(F32)
+        squares += jnp.sum(wide * wide, -1, keepdims=True)
+    inverse = lax.rsqrt(squares * (1.0 / WIDTH) + 1e-06)
+
+    def back(k):
+        return remote(
+            back_leaving.at[k], back_landed.at[k], back_send.at[k], back_recv.at[k], place.earlier
+        )
 
     @pl.when(section == 7)
     def _():
         for k in range(CH):
-            landed[k] = jnp.zeros((ROWS, CW), BF16)
-
+            back_landed[k] = jnp.zeros((ROWS, CW), BF16)
+
+    grad_att_cols = slice(WIDTH, WIDTH + HD)
     for k in range(CH):
         @pl.when(section < 7)
         def _():
-            hop(k).wait_recv()
-
-        grad = (landed[k].astype(F32) + hint_ref[k]).astype(BF16)
+            back(k).wait_recv()
+
+        grad = (back_landed[k].astype(F32) + acc[:, k * CW : (k + 1) * CW]).astype(BF16)
         after[k] = grad
-        part = dot(grad, wout_ref[:, k * CW : (k + 1) * CW], ((1,), (1,)))
+        part = dot(grad, out[:, k * CW : (k + 1) * CW], ((1,), (1,)))
         if k == 0:
-            acc[...] = part
+            acc[:, grad_att_cols] = part
         else:
-            acc[...] += part
+            acc[:, grad_att_cols] += part
     through = jnp.zeros((ROWS, 1), F32)
     for h in range(HEADS):
         lo = h * HEAD
-        grad_att = acc[:, lo : lo + HEAD].astype(BF16)
-        queries = proj_ref[:, lo : lo + HEAD]
-        keys = proj_ref[:, HD + lo : HD + lo + HEAD]
-        values = proj_ref[:, 2 * HD + lo : 2 * HD + lo + HEAD]
-        probs = probs_ref[h]
+        grad_att = acc[:, WIDTH + lo : WIDTH + lo + HEAD].astype(BF16)
+        queries = proj[:, lo : lo + HEAD]
+        keys = proj[:, HD + lo : HD + lo + HEAD]
+        values = proj[:, 2 * HD + lo : 2 * HD + lo + HEAD]
+        soft = probs[h]
         grad_probs = dot(grad_att, values, ((1,), (1,)))
-        grad_values = dot(probs.astype(BF16), grad_att, ((0,), (0,))).astype(BF16)
-        total = jnp.sum(grad_probs * probs, -1, keepdims=True)
-        grad_scores = (probs * (grad_probs - total) * SCALE).astype(BF16)
+        grad_values = dot(soft.astype(BF16), grad_att, ((0,), (0,))).astype(BF16)
+        total = jnp.sum(grad_probs * soft, -1, keepdims=True)
+        grad_scores = (soft * (grad_probs - total) * SCALE).astype(BF16)
         grad_queries = dot(grad_scores, keys).astype(BF16)
         grad_keys = dot(grad_scores, queries, ((0,), (0,))).astype(BF16)
         for n, (grad, value) in enumerate(
@@ -606,38 +714,78 @@
     def _():
         grad_proj = gproj[...]
         for k in range(CH):
-            grad_normed = dot(grad_proj, wqkv_ref[k * CW : (k + 1) * CW, :], ((1,), (1,)))
-            value = after[k].astype(F32) + inverse * grad_normed - control_ref[k].astype(F32) * slope
-            leaving[k] = value.astype(BF16)
-            hop(k).start()
-
+            grad_normed = dot(grad_proj, qkv[k * CW : (k + 1) * CW, :], ((1,), (1,)))
+            value = after[k].astype(F32) + inverse * grad_normed - landed[k].astype(F32) * slope
+            back_leaving[k] = value.astype(BF16)
+            back(k).start()
+
+    @pl.when(core == 1)
+    def _():
+        transposes()
+
+    qkv_gather.wait_sent()
+    out_gather.wait_sent()
     for m in range(CH):
         rows = slice(m * CW, (m + 1) * CW)
         for n in range(3):
             cols = slice(n * HD, (n + 1) * HD)
-            grad_qkv[rows, cols] = dot(normed_t[rows, :], gproj[:, cols]).astype(BF16)
+            qkv[rows, cols] = dot(normed_t[rows, :], gproj[:, cols]).astype(BF16)
     for m in range(HD // CW):
         rows = slice(m * CW, (m + 1) * CW)
         for n in range(CH):
-            grad_out[rows, n * CW : (n + 1) * CW] = dot(att_t[rows, :], after[n]).astype(BF16)
+            out[rows, n * CW : (n + 1) * CW] = dot(att_t[rows, :], after[n]).astype(BF16)
     reduce([red_qkv, red_out])
 
     @pl.when(core == 1)
     def _():
         hint_part()
 
-    red_qkv.put(sum_qkv)
-    red_out.put(sum_out)
-    red_hint.put(sum_hint)
-
-    @pl.when(section > 0)
+    keeps = [
+        red.put(ref, out_sem.at[i])
+        for i, (red, ref) in enumerate(((red_qkv, sum_qkv), (red_out, sum_out), (red_hint, sum_hint)))
+    ]
+
+    @pl.when(kept)
+    def _():
+        member_copy().wait_send()
+        for copy in row_copies(True):
+            copy.wait_send()
+        for by in (2, 1, 3):
+            mine_copy(by, 0, section).wait_send()
+        mine_across().wait_send()
+
+    @pl.when(place.moved)
+    def _():
+        permitted_copy().wait_send()
+        update_across().wait_send()
+
+    @pl.when(section < 7)
     def _():
         for k in range(CH):
             hop(k).wait_send()
 
-    red_qkv.wait_sent()
-    red_out.wait_sent()
-    red_hint.wait_sent()
+    @pl.when(section > 0)
+    def _():
+        for k in range(CH):
+            back(k).wait_send()
+
+    for by in far_first:
+        for half in range(2):
+            term_copy(by, half).wait_send()
+        gs_copy(by, section).wait_send()
+    for red in (red_qkv, red_out, red_hint):
+        red.wait_sent()
+    mine_keep.wait()
+    for keep in keeps:
+        keep()
+
+
+def scale_kernel(mine_ref, gain_ref, qkv_ref, out_ref, hint_ref, features, qkv, out, hint):
+    mine = mine_ref[...].astype(F32)
+    inverse = lax.rsqrt(jnp.mean(mine * mine, -1, keepdims=True) + 1e-06)
+    features[...] = mine * inverse * gain_ref[...]
+    for src, dst in ((qkv_ref, qkv), (out_ref, out), (hint_ref, hint)):
+        dst[...] = src[...].astype(F32) * 4096.0 ** (-0.5)
 
 
 def dma_sems(*shape):
@@ -659,23 +807,6 @@
     )
 
 
-def chunked(value):
-    return value.reshape(ROWS, CH, CW).transpose(1, 0, 2)
-
-
-def flat(value):
-    return value.transpose(1, 0, 2).reshape(ROWS, WIDTH)
-
-
-def swap_roles(value):
-    return lax.ppermute(value, ("xlo", "core"), [(0, 0), (1, 2), (2, 1), (3, 3)])
-
-
-def of_clip(value):
-    other = lax.ppermute(value, "core", [(0, 1), (1, 0)])
-    return jnp.where(lax.axis_index("core") == lax.axis_index("xlo"), value, other)
-
-
 def tile_members(layout):
     holds = layout[None, :] == jnp.arange(ROWS)[:, None]
     tile_of = jnp.sum(jnp.where(holds, jnp.arange(ROWS)[None, :] // TILE, 0), 1)
@@ -701,106 +832,68 @@
     member = tile_members(token_layout[0])
     permitted = permitted_tiles(window_offset[0], tile_mask[0])
     chunks = (CH, ROWS, CW)
-
-    control_s, control_next, proj, att, bias, term, weight_qkv, weight_out, weight_hint = kernel_call(
-        forward_kernel,
-        "avvaaa",
+    gain = out_gain[None]
+    mine, sum_qkv, sum_out, sum_hint = kernel_call(
+        section_kernel,
+        "avvaaaaaav",
         [
-            (shape_of(*chunks), "v"),
-            (shape_of(*chunks), "v"),
-            (shape_of(ROWS, QKV), "v"),
-            (shape_of(ROWS, HD), "v"),
-            (shape_of(ROWS, ROWS, dtype=F32), "v"),
-            (shape_of(ROWS, FEAT, dtype=F32), "v"),
-            (shape_of(WIDTH, QKV), "a"),
-            (shape_of(HD, WIDTH), "a"),
-            (shape_of(WIDTH, FEAT), "a"),
+            (shape_of(ROWS, FEAT), "a"),
+            (shape_of(96, QKV), "a"),
+            (shape_of(48, WIDTH), "a"),
+            (shape_of(96, FEAT), "a"),
         ],
         [
-            pltpu.VMEM(chunks, BF16),
-            pltpu.VMEM(chunks, BF16),
+            *[pltpu.VMEM(chunks, BF16)] * 5,
             pltpu.VMEM((ROWS, QKV), F32),
+            pltpu.VMEM((ROWS, QKV), BF16),
+            pltpu.VMEM((ROWS, HD), BF16),
+            pltpu.VMEM((ROWS, QKV), BF16),
+            pltpu.VMEM((HEADS, ROWS, ROWS), F32),
+            pltpu.VMEM((ROWS, ROWS), F32),
             pltpu.VMEM((ROWS, 128), BF16),
             pltpu.VMEM((128, 128), BF16),
             pltpu.VMEM((WIDTH, QKV), BF16),
             pltpu.VMEM((HD, WIDTH), BF16),
             pltpu.VMEM((WIDTH, FEAT), BF16),
-            dma_sems(CH), dma_sems(CH), dma_sems(2), dma_sems(2), dma_sems(CH), dma_sems(3),
-            dma_sems(2, 21), dma_sems(2, 21), dma_sems(2),
-            dma_sems(2, 21), dma_sems(2, 21), dma_sems(2),
-            dma_sems(2, 21), dma_sems(2, 21), dma_sems(2),
-            pltpu.SemaphoreType.REGULAR,
-        ],
-        1,
-        100_000_000_000,
-    )(control_in, member, permitted, w_qkv[0], w_out[0], w_hint[0])
-
-    base = of_clip(base_in)
-    cot = of_clip(cotangent)
-    update = swap_roles(base_update[0])
-    term = term + update.astype(F32)
-    summed = base.astype(F32) + lax.psum(term.astype(BF16), ("z", "core")).astype(F32)
-
-    inverse = lax.rsqrt(jnp.mean(summed * summed, -1, keepdims=True) + 1e-06)
-    grad_normed = cot.astype(F32) * out_gain
-    grad_summed = (
-        inverse * grad_normed
-        - summed * inverse**3 * jnp.mean(grad_normed * summed, -1, keepdims=True)
-    ).astype(BF16)
-
-    mine = swap_roles(summed.astype(BF16)).astype(F32)
-    features = mine * lax.rsqrt(jnp.mean(mine * mine, -1, keepdims=True) + 1e-06) * out_gain
-
-    hint_grad = dot(grad_summed, weight_hint, ((1,), (1,)))
-
-    sum_qkv, sum_out, sum_hint = kernel_call(
-        backward_kernel,
-        "vvvvvvvvv",
-        [
-            (shape_of(96, QKV), "v"),
-            (shape_of(48, WIDTH), "v"),
-            (shape_of(96, FEAT), "v"),
-        ],
-        [
-            pltpu.VMEM(chunks, BF16),
-            pltpu.VMEM(chunks, BF16),
-            pltpu.VMEM((HEADS, ROWS, ROWS), F32),
-            pltpu.VMEM((ROWS, HD), F32),
-            pltpu.VMEM(chunks, BF16),
-            pltpu.VMEM((ROWS, QKV), BF16),
             pltpu.VMEM((WIDTH, ROWS), BF16),
             pltpu.VMEM((HD, ROWS), BF16),
-            pltpu.VMEM((WIDTH, ROWS), BF16),
-            pltpu.VMEM((WIDTH, QKV), BF16),
-            pltpu.VMEM((HD, WIDTH), BF16),
-            pltpu.VMEM((WIDTH, FEAT), BF16),
+            pltpu.VMEM((ROWS, FEAT), BF16),
+            pltpu.VMEM((8, 32, FEAT), BF16),
+            pltpu.VMEM((ROWS, FEAT), BF16),
+            pltpu.VMEM((ROWS, FEAT), BF16),
+            *[pltpu.VMEM((32, FEAT), BF16)] * 3,
             pltpu.VMEM((2, 15, 96, QKV // 2), BF16),
             pltpu.VMEM((2, 15, 48, WIDTH // 2), BF16),
             pltpu.VMEM((2, 15, 96, FEAT // 2), BF16),
             pltpu.VMEM((96, QKV), BF16),
             pltpu.VMEM((48, WIDTH), BF16),
             pltpu.VMEM((96, FEAT), BF16),
-            pltpu.VMEM((96, QKV), BF16),
-            pltpu.VMEM((48, WIDTH), BF16),
-            pltpu.VMEM((96, FEAT), BF16),
-            dma_sems(CH), dma_sems(CH),
-            dma_sems(2, 21), dma_sems(2, 21),
-            dma_sems(2, 21), dma_sems(2, 21),
-            dma_sems(2, 21), dma_sems(2, 21),
+            *[dma_sems(CH)] * 4,
+            dma_sems(5), dma_sems(5), dma_sems(CH), dma_sems(3), dma_sems(4),
+            *[dma_sems(2, 21), dma_sems(2, 21), dma_sems(2)] * 3,
+            *[dma_sems(2, 21)] * 6,
+            dma_sems(8, 2), dma_sems(8, 2), dma_sems(8), dma_sems(8), dma_sems(5), dma_sems(5, 2),
+            pltpu.SemaphoreType.REGULAR,
         ],
-        2,
+        1,
         100_000_000_000,
     )(
-        chunked(hint_grad), control_s, proj, bias, weight_qkv, weight_out, att, control_next,
-        grad_summed,
+        control_in, member, permitted, w_qkv[0], w_out[0], w_hint[0],
+        base_in, cotangent, base_update[0], gain,
     )
-    factor = 4096.0 ** (-0.5)
-    return (
-        features,
-        (sum_qkv.astype(F32) * factor)[None],
-        (sum_out.astype(F32) * factor)[None],
-        (sum_hint.astype(F32) * factor)[None],
-    )
+    features, grad_qkv, grad_out, grad_hint = pl.pallas_call(
+        scale_kernel,
+        out_shape=[
+            shape_of(ROWS, FEAT, dtype=F32),
+            shape_of(96, QKV, dtype=F32),
+            shape_of(48, WIDTH, dtype=F32),
+            shape_of(96, FEAT, dtype=F32),
+        ],
+        in_specs=[pl.BlockSpec(memory_space=pltpu.VMEM)] * 5,
+        out_specs=[pl.BlockSpec(memory_space=pltpu.VMEM)] * 4,
+        compiler_params=pltpu.CompilerParams(vmem_limit_bytes=VMEM_LIMIT // 2),
+    )(mine, gain, sum_qkv, sum_out, sum_hint)
+    return features, grad_qkv[None], grad_out[None], grad_hint[None]
 
 
 def solution(mesh):

time: 463 us -> 359 us (0.78)
  waiting for transfers between devices: 105 us -> 0 us
  Pallas kernels: 312 us -> 350 us
  other arithmetic: 19.6 us -> 2.91 us
  between operations: 14.2 us -> 0.67 us
  starting transfers between devices: 7.04 us -> 0 us
    psum x1 -> x0, waiting for transfers between devices: 92.1 us -> none  [shards(): lax.psum(term.astype(BF16), ('z', 'core')).astype(F32)]
    pallas_call x2, Pallas kernels: 312 us -> 350 us  [the longest x1 347 us: shards(): kernel_call(section_kernel, 'avvaaaaaav', [(shape_of(ROWS, FEAT), 'a'), (...]
    ppermute x4 -> x0, waiting for transfers between devices: 13 us -> none  [the longest x2 13 us: swap_roles(): lax.ppermute(value, ('xlo', 'core'), [(0, 0), (1, 2), (2, 1), (3, 3)])]
    ppermute x4 -> x0, starting transfers between devices: 7 us -> none  [the longest x2 6.42 us: swap_roles(): lax.ppermute(value, ('xlo', 'core'), [(0, 0), (1, 2), (2, 1), (3, 3)])]
    broadcast_in_dim x3 -> x0, other arithmetic: 5.69 us -> none  [the longest x1 2.06 us: shards(): (sum_hint.astype(F32) * factor)[None]]
    convert_element_type x2 -> x0, other arithmetic: 5.66 us -> none  [the longest x1 3.56 us: shards(): term.astype(BF16)]
  transfers between devices with their start and end apart: 5 -> 0, of which waited for: 2 -> 0; matrix products, arithmetic and copies ran while one was open for 2% -> 0% of each run, Pallas kernels for 33% -> 0%
where the time goes in v3:
time: 359 us
  Pallas kernels  350 us (97%)
  local copies, waits for them, and re-layouts  5.58 us (2%)
    pallas_call x1, Pallas kernels, shards(): kernel_call(section_kernel, 'avvaaaaaav', [(shape_of(ROWS, FEAT), 'a'), (...  347 us

profile of v3, /device:TPU:1, one launch (start us, length us, event | category | flops | bytes accessed | tf_op | source)
XLA Modules:
  0.0 358.9 jit_solution(10479488121860027060)
XLA Ops:
  0.6 0.8 fusion.2
  1.4 0.8 select_reduce_fusion
  2.2 1.3 broadcast_in_dim.32.gain_ref
  3.5 0.6 pad_convert_fusion.permitted_ref
  4.1 0.7 fusion.member_ref
  4.9 0.0 copy-start.4
  4.9 347.2 %shard_map.138 = (bf16[256,2560]{1,0:T(8,128)(2,1)}, bf16[96,2304]{1,0:T(8,128)(2,1)}, bf16[48,1536]{1,0:T(8,128)(2,1)}, bf16[96,2560]{1,0:T(8,128)(2,1)}) custom-call(bf16[256,1536]{1,0:T(8,128)(2,1)} %start_ref.1, bf16[256,128]{1,0:T(8,128)(2,1)} %fusion.member_ref, bf16[128,128]{1,0:T(8,128)(2,1)} %pad_convert_fusion.permitted_ref, ...), custom_call_target="tpu_custom_call" | custom-call | flops 99999997952 | bytes 12000000 | tf_op jit(solution)/shard_map/pallas_call | solution.py:836
  352.0 0.0 copy-done.4
  352.0 0.0 copy-start
  352.1 1.3 copy-done
  353.4 0.0 copy-start.1
  353.4 1.0 copy-done.1
  354.4 0.0 copy-start.2
  354.4 1.0 copy-done.2
  355.4 0.0 copy-start.3
  355.4 0.9 copy-done.3
  356.3 2.6 shard_map.139
  (1 shorter events, 0.0 us)
Async XLA Ops:
  4.9 347.2 %copy-start.4 = (f32[1,2560]{1,0:T(1,128)S(1)}, f32[1,2560]{1,0:T(1,128)}, u32[]{:S(2)}) copy-start(f32[1,2560]{1,0:T(1,128)} %broadcast_in_dim.32.gain_ref) | copy-start | bytes 30724
  352.0 1.3 copy-start
  353.4 1.0 copy-start.1
  354.4 1.0 copy-start.2
  355.4 0.9 copy-start.3
